TPU v7x, 32 devices: a whole 2x2x4 slice. The times are simulated.
32 devices in a mesh: dom: 16 (over z, y, core), feat: 2 (over x).
Axes of the slice: x: 2, y: 2, z: 4, core: 2. Of those that a mesh axis runs over, the one named last changes fastest.
Arguments:
- node_features: bfloat16 [16384, 128], P('dom'), may hold values from -6 to 6
- weight: bfloat16 [128, 256], P(None, 'feat'), may hold values from -0.5 to 0.5
- bias: float32 [256], P('feat'), may hold values from -3 to 3
- tile_values: bfloat16 [1536, 128, 128], P('dom')
- tile_src: int32 [1536], P('dom'), may hold values from 0 to 7
- tile_dst: int32 [1536], P('dom'), may hold values from 0 to 31, as said below
- tile_counts: int32 [16], P('dom'), may hold values from 4 to 96
- out_grad: bfloat16 [16384, 256], P('dom', 'feat'), may hold values from -6 to 6
Outputs:
- output: bfloat16 [16384, 256], P('dom', 'feat')
- weight_grad: float32 [128, 256], P(None, 'feat')
- bias_grad: float32 [256], P('feat')
- input_grad: bfloat16 [16384, 128], P('dom', 'feat')
Inputs may be any that keep to these rules, and one draw needn't show every extreme that they name: The partition offset tile_dst[k] // 8 of slot k of a partition equals k mod 4.
All inputs are finite; a program needn't handle non-finite values.
Results may differ from a plain program's by a relative error of at most 0.0075.
Values may be sent and summed in bfloat16 or wider, within the bound.
No kernel may reach another device: no remote copies, remote signals or barrier semaphores. Data moves between devices by JAX's collectives and lax.ppermute only.
A program may use at most 64 MiB of HBM per device.

v0:
```python
import functools

import jax
import jax.numpy as jnp
from jax import lax
from jax.experimental import pallas as pl
from jax.experimental.pallas import tpu as pltpu
from jax.sharding import PartitionSpec as P

BLOCK = 128
REACH = 4
F32 = jnp.float32
BF16 = jnp.bfloat16
VMEM = pl.BlockSpec(memory_space=pltpu.VMEM)
SMEM = pl.BlockSpec(memory_space=pltpu.SMEM)
HBM = pl.BlockSpec(memory_space=pltpu.HBM)


def call(kernel, out_shape, in_specs, scratch=(), flops=0):
    return pl.pallas_call(
        kernel,
        out_shape=out_shape,
        in_specs=in_specs,
        out_specs=[VMEM] * len(out_shape),
        scratch_shapes=list(scratch),
        compiler_params=pltpu.CompilerParams(vmem_limit_bytes=24 * 1024 * 1024),
        cost_estimate=pl.CostEstimate(flops=flops, bytes_accessed=2**20, transcendentals=0),
    )


def groups_at_once(groups):
    return next(m for m in (4, 3, 2, 1) if groups % m == 0)


def in_hbm(a):
    return pltpu.with_memory_space_constraint(a, pltpu.HBM)


def own_core():
    return lax.rem(lax.axis_index("dom"), 2)


def slot_loop(count, groups, offsets, body, arrive=None):
    m = groups_at_once(groups)

    def chunk(i, carry):
        if arrive is not None:
            arrive(i)

        @pl.when(i * (m * REACH) < count)
        def _():
            for u in range(m):
                for o in offsets:
                    j = i * m + u
                    body(j, o, j * REACH + o < count)

        return carry

    lax.fori_loop(0, groups // m, chunk, 0)


def push(xt, tiles_ref, src_ref, dst_ref, j, o, live, acc):
    blocks = xt.shape[0]
    k = j * REACH + o
    d = jnp.where(live, dst_ref[k] - o * blocks, blocks)
    acc[d] += lax.dot_general(
        xt[src_ref[k]], tiles_ref[j, o], (((1,), (1,)), ((), ())), preferred_element_type=F32
    )


def forward_far_kernel(
    count, src_hbm, dst_hbm, x_hbm, tiles_hbm, tiles, xt, direct, swap, x, src, dst, acc1, acc3, small, large
):
    blocks, width, _ = xt.shape
    groups = tiles.shape[0]
    m = groups_at_once(groups)
    copies = [
        pltpu.make_async_copy(a, b, small.at[i])
        for i, (a, b) in enumerate(((x_hbm, x), (src_hbm, src), (dst_hbm, dst)))
    ]

    def chunk(i):
        part = pl.ds(i * m, m)
        return pltpu.make_async_copy(tiles_hbm.at[part], tiles.at[part], large.at[i])

    for c in copies:
        c.start()
    for i in range(groups // m):
        chunk(i).start()
    for a in (acc1, acc3):
        a[...] = jnp.zeros_like(a)
    row = lax.broadcasted_iota(jnp.int32, (width, x.shape[1]), 0)
    column = lax.broadcasted_iota(jnp.int32, (width, x.shape[1]), 1)
    pick = (column == row + lax.axis_index("feat") * width).astype(BF16)
    for c in copies:
        c.wait()
    for b in range(blocks):
        xt[b] = lax.dot_general(
            pick, x[b * BLOCK : (b + 1) * BLOCK, :], (((1,), (1,)), ((), ())), preferred_element_type=F32
        ).astype(BF16)

    def body(j, o, live):
        push(xt, tiles, src, dst, j, o, live, acc1 if o == 1 else acc3)

    slot_loop(count[0], groups, (1, 3), body, lambda i: chunk(i).wait())
    first = own_core() == 0

    @pl.when(first)
    def _():
        direct[...] = acc1[:blocks].astype(BF16)
        swap[...] = acc3[:blocks].astype(BF16)

    @pl.when(jnp.logical_not(first))
    def _():
        direct[...] = acc3[:blocks].astype(BF16)
        swap[...] = acc1[:blocks].astype(BF16)


def forward_near_kernel(count, src, dst, xt, tiles, acc0, acc2):
    for a in (acc0, acc2):
        a[...] = jnp.zeros_like(a)

    def body(j, o, live):
        push(xt, tiles, src, dst, j, o, live, acc2 if o == 2 else acc0)

    slot_loop(count[0], tiles.shape[0], (2, 0), body)


def sum_kernel(n, *refs):
    out = refs[n]
    blocks = out.shape[0]
    total = refs[0][:blocks].astype(F32)
    for r in refs[1:n]:
        total = total + r[:blocks].astype(F32)
    out[...] = total.astype(out.dtype)


def middle_kernel(parts, bias_ref, w_ref, og_ref, *refs):
    h_refs, (out_ref, ht, grads), g_refs = refs[:parts], refs[parts : parts + 3], refs[parts + 3 :]
    blocks, width, _ = h_refs[0].shape
    f_in = w_ref.shape[0]
    me = lax.axis_index("feat")
    for q in range(parts):
        row = pl.multiple_of(lax.rem(me + q, parts) * width, width)
        for b in range(blocks):
            ht[pl.ds(row, width), b * BLOCK : (b + 1) * BLOCK] = h_refs[q][b]
    ht[f_in:, :] = jnp.ones((ht.shape[0] - f_in, ht.shape[1]), BF16)
    for b in range(blocks):
        rows = slice(b * BLOCK, (b + 1) * BLOCK)
        pre = lax.dot_general(
            ht[:f_in, rows], w_ref[...], (((0,), (0,)), ((), ())), preferred_element_type=F32
        ) + bias_ref[...]
        s = jax.nn.sigmoid(pre)
        out_ref[rows, :] = (pre * s).astype(BF16)
        grad = (og_ref[rows, :].astype(F32) * s * (1.0 + pre * (1.0 - s))).astype(BF16)
        grads[rows, :] = grad
        for q in range(parts):
            row = pl.multiple_of(lax.rem(me + q, parts) * width, width)
            g_refs[q][b] = lax.dot_general(
                w_ref[pl.ds(row, width), :], grad, (((1,), (1,)), ((), ())), preferred_element_type=F32
            ).astype(g_refs[q].dtype)


def weight_grad_kernel(ht, grads, out):
    full = jnp.dot(ht[...], grads[...], preferred_element_type=F32)
    out[...] = full[: out.shape[0]]


def pull(g, tiles, src, dst, j, o, live, acc):
    blocks = g.shape[0]
    k = j * REACH + o
    s = jnp.where(live, src[k], blocks)
    acc[s] += jnp.dot(g[dst[k] - o * blocks], tiles[j, o], preferred_element_type=F32)


def backward_own_kernel(count, src, dst, tiles, g0, acc):
    acc[...] = jnp.zeros_like(acc)
    slot_loop(
        count[0], tiles.shape[0], (0,), lambda j, o, live: pull(g0, tiles, src, dst, j, o, live, acc)
    )


def backward_near_kernel(count, src, dst, tiles, g2, gd, acc2, accd):
    acc2[...] = jnp.zeros_like(acc2)
    accd[...] = jnp.zeros_like(accd)
    far = 1 + 2 * own_core()

    def body(j, o, live):
        if o == 2:
            pull(g2, tiles, src, dst, j, o, live, acc2)
        else:
            pull(gd, tiles, src, dst, j, far, j * REACH + far < count[0], accd)

    slot_loop(count[0], tiles.shape[0], (2, 1), body)


def backward_last_kernel(count, src, dst, tiles, g, acc0, acc2, accd, out, acc):
    blocks = g.shape[0]
    acc[...] = jnp.zeros_like(acc)
    far = 3 - 2 * own_core()
    slot_loop(
        count[0],
        tiles.shape[0],
        (0,),
        lambda j, o, live: pull(g, tiles, src, dst, j, far, j * REACH + far < count[0], acc),
    )
    for b in range(blocks):
        total = acc[b] + acc0[b] + acc2[b] + accd[b]
        out[:, b * BLOCK : (b + 1) * BLOCK] = total.astype(BF16)


def moved(block, axis, target):
    n = lax.axis_size(axis)
    return lax.ppermute(block, axis, [(i, target(i) % n) for i in range(n)])


def radices(n):
    out = []
    while n > 1:
        r = 2 if n % 2 == 0 else n
        out.append(r)
        n //= r
    return out


def sum_step(part, axis, stride, r):
    def target(step, i):
        digit = i // stride % r
        return i + ((digit + step) % r - digit) * stride

    received = [moved(part, axis, functools.partial(target, s)) for s in range(1, r)]
    for other in received:
        part = part + other
    return part


def shards(node_features, weight, bias, tile_values, tile_src, tile_dst, tile_counts, out_grad):
    nodes, f_in = node_features.shape
    hid = weight.shape[1]
    blocks = nodes // BLOCK
    parts = lax.axis_size("feat")
    width = f_in // parts
    capacity = tile_values.shape[0]
    groups = capacity // REACH
    piece = jax.ShapeDtypeStruct((blocks, width, BLOCK), BF16)
    wide = jax.ShapeDtypeStruct((blocks, width, BLOCK), F32)
    totals = jax.ShapeDtypeStruct((blocks + 1, width, BLOCK), F32)
    acc = pltpu.VMEM(totals.shape, F32)
    tiles = jax.ShapeDtypeStruct((groups, REACH, BLOCK, BLOCK), BF16)
    m = groups_at_once(groups)
    flops = 2 * capacity * BLOCK * BLOCK * width // REACH
    index = (tile_counts, tile_src, tile_dst)

    def swapped(i):
        return i ^ 1

    tiles, xt, direct, swap = call(
        forward_far_kernel,
        [tiles, piece, piece, piece],
        [SMEM] + [HBM] * 4,
        [
            pltpu.VMEM(node_features.shape, BF16),
            pltpu.SMEM((capacity,), jnp.int32),
            pltpu.SMEM((capacity,), jnp.int32),
            acc,
            acc,
            pltpu.SemaphoreType.DMA((3,)),
            pltpu.SemaphoreType.DMA((groups // m,)),
        ],
        2 * flops,
    )(tile_counts, *(in_hbm(a) for a in (tile_src, tile_dst, node_features, tile_values.reshape(tiles.shape))))
    swap = moved(swap, "dom", swapped)
    direct = moved(direct, "dom", lambda i: i + 1 + 2 * (i % 2))
    acc0, acc2 = call(forward_near_kernel, [totals, totals], [SMEM] * 3 + [VMEM] * 2, (), 2 * flops)(
        *index, xt, tiles
    )
    (chip,) = call(functools.partial(sum_kernel, 2), [piece], [VMEM] * 2)(acc2, swap)
    chip = moved(chip, "dom", lambda i: i + 2)
    (h,) = call(functools.partial(sum_kernel, 3), [piece], [VMEM] * 3)(acc0, direct, chip)
    hs = [h] + [moved(h, "feat", lambda i, q=q: i - q) for q in range(1, parts)]
    output, ht, grads, g_own, *g_others = call(
        functools.partial(middle_kernel, parts),
        [
            jax.ShapeDtypeStruct((nodes, hid), BF16),
            jax.ShapeDtypeStruct((f_in + 16, nodes), BF16),
            jax.ShapeDtypeStruct((nodes, hid), BF16),
            wide,
        ]
        + [piece] * (parts - 1),
        [VMEM] * (3 + parts),
        (),
        4 * nodes * f_in * hid,
    )(bias.reshape(1, hid), weight, out_grad, *hs)
    g_received = [moved(g, "feat", lambda i, q=q + 1: i + q) for q, g in enumerate(g_others)]
    (wg,) = call(
        weight_grad_kernel,
        [jax.ShapeDtypeStruct((f_in + 8, hid), F32)],
        [VMEM] * 2,
        (),
        2 * nodes * f_in * hid,
    )(ht, grads)
    (g,) = call(functools.partial(sum_kernel, parts), [piece], [VMEM] * parts)(g_own, *g_received)
    stride, *steps = radices(lax.axis_size("dom"))
    wg = sum_step(wg, "dom", 1, stride)
    g, wg = lax.optimization_barrier((g, wg))
    g_chip = moved(g, "dom", lambda i: i - 2)
    g_direct = moved(g, "dom", lambda i: i - 3 + 2 * (i % 2))
    (back0,) = call(backward_own_kernel, [totals], [SMEM] * 3 + [VMEM] * 2, (), flops)(*index, tiles, g)
    g_swap = moved(g_chip, "dom", swapped)
    back2, backd = call(backward_near_kernel, [totals, totals], [SMEM] * 3 + [VMEM] * 3, (), 2 * flops)(
        *index, tiles, g_chip, g_direct
    )
    (input_grad,) = call(
        backward_last_kernel,
        [jax.ShapeDtypeStruct((width, nodes), BF16)],
        [SMEM] * 3 + [VMEM] * 5,
        [acc],
        flops,
    )(*index, tiles, g_swap, back0, back2, backd)
    for r in steps:
        wg = sum_step(wg, "dom", stride, r)
        stride *= r
    return output, wg[:f_in], wg[f_in], input_grad.T


def solution(mesh):
    return jax.shard_map(
        shards,
        mesh=mesh,
        in_specs=(
            P("dom", None),
            P(None, "feat"),
            P("feat"),
            P("dom", None, None),
            P("dom"),
            P("dom"),
            P("dom"),
            P("dom", "feat"),
        ),
        out_specs=(P("dom", "feat"), P(None, "feat"), P("feat"), P("dom", "feat")),
        check_vma=False,
    )
```

profile of v0, /device:TPU:0, one launch (start us, length us, event | category | flops | bytes accessed | tf_op | source)
XLA Modules:
  0.0 47.8 jit_solution(12252402114590039514)
XLA Ops:
  1.3 2.7 %shard_map.111 = (bf16[24,4,128,128]{3,2,1,0:T(8,128)(2,1)S(1)}, bf16[8,64,128]{2,1,0:T(8,128)(2,1)S(1)}, bf16[8,64,128]{2,1,0:T(8,128)(2,1)S(1)}, bf16[8,64,128]{2,1,0:T(8,128)(2,1)S(1)}) custom-call(s32[1]{0:T(128)S(6)} %copy.12.count, s32[96]{0:T(128)} %src.7, s32[96]{0:T(128)} %dst.7, bf16[1024,128]{1,0:T(8,128)(2,1)} %x_hbm.1, ...), custom_call_target="tpu_custom_call" | custom-call | flops 100663296 | bytes 1048576 | tf_op jit(solution)/shard_map/pallas_call | solution.py:257
  4.1 0.5 %collective-permute-start.1 = (bf16[8,64,128]{2,1,0:T(8,128)(2,1)S(1)}, bf16[8,64,128]{2,1,0:T(8,128)(2,1)S(1)}, u32[]{:S(2)}, u32[]{:S(2)}) collective-permute-start(bf16[8,64,128]{2,1,0:T(8,128)(2,1)S(1)} %get-tuple-element.24), channel_id=1, source_target_pairs={{0,2},{2,0},{4,6},{6,4},{8,10},{10,8},{12,14},{14,12},{16,18},{18,... | collective-permute-start | bytes 393224 | tf_op jit(solution)/shard_map/ppermute | solution.py:214
  4.7 1.4 %shard_map.112 = (f32[9,64,128]{2,1,0:T(8,128)S(1)}, f32[9,64,128]{2,1,0:T(8,128)S(1)}) custom-call(s32[1]{0:T(128)S(6)} %copy.12.count, s32[96]{0:T(128)S(1)} %copy-done.2, s32[96]{0:T(128)S(1)} %copy-done.3, bf16[8,64,128]{2,1,0:T(8,128)(2,1)S(1)} %get-tuple-element.19.xt, bf16[24,4,128,128]{3,2,1,0:T(8,128)(2,1)S(1)} %get-tuple-element.20.tiles), custom_call_target="tpu_custom_call" | custom-call | flops 100663296 | bytes 1048576 | tf_op jit(solution)/shard_map/pallas_call | solution.py:274
  6.2 3.0 %collective-permute-start.2 = (bf16[8,64,128]{2,1,0:T(8,128)(2,1)S(1)}, bf16[8,64,128]{2,1,0:T(8,128)(2,1)S(1)}, u32[]{:S(2)}, u32[]{:S(2)}) collective-permute-start(bf16[8,64,128]{2,1,0:T(8,128)(2,1)S(1)} %shard_map.113), channel_id=1, source_target_pairs={{0,4},{2,6},{4,8},{6,10},{8,12},{10,14},{12,16},{14,18},{16,20},{1... | collective-permute-start | bytes 393224 | tf_op jit(solution)/shard_map/ppermute | solution.py:214
  9.2 2.8 %collective-permute-done.refs_1_ = bf16[8,64,128]{2,1,0:T(8,128)(2,1)S(1)} collective-permute-done((bf16[8,64,128]{2,1,0:T(8,128)(2,1)S(1)}, bf16[8,64,128]{2,1,0:T(8,128)(2,1)S(1)}, u32[]{:S(2)}, u32[]{:S(2)}) %collective-permute-start) | collective-permute-done | bytes 131104 | tf_op jit(solution)/shard_map/ppermute | solution.py:214
  12.0 3.4 %collective-permute-done.2.refs_2_ = bf16[8,64,128]{2,1,0:T(8,128)(2,1)S(1)} collective-permute-done((bf16[8,64,128]{2,1,0:T(8,128)(2,1)S(1)}, bf16[8,64,128]{2,1,0:T(8,128)(2,1)S(1)}, u32[]{:S(2)}, u32[]{:S(2)}) %collective-permute-start.2) | collective-permute-done | bytes 131104 | tf_op jit(solution)/shard_map/ppermute | solution.py:214
  15.4 2.9 %collective-permute-start.3 = (bf16[8,64,128]{2,1,0:T(8,128)(2,1)S(1)}, bf16[8,64,128]{2,1,0:T(8,128)(2,1)S(1)}, u32[]{:S(2)}, u32[]{:S(2)}) collective-permute-start(bf16[8,64,128]{2,1,0:T(8,128)(2,1)S(1)} %shard_map.114.refs_0_), channel_id=1, source_target_pairs={{0,1},{1,0},{2,3},{3,2},{4,5},{5,4},{6,7},{7,6},{8,9},{9,8},{10,11... | collective-permute-start | bytes 393224 | tf_op jit(solution)/shard_map/ppermute | solution.py:214
  18.3 3.8 %collective-permute-done.3.refs_1_ = bf16[8,64,128]{2,1,0:T(8,128)(2,1)S(1)} collective-permute-done((bf16[8,64,128]{2,1,0:T(8,128)(2,1)S(1)}, bf16[8,64,128]{2,1,0:T(8,128)(2,1)S(1)}, u32[]{:S(2)}, u32[]{:S(2)}) %collective-permute-start.3) | collective-permute-done | bytes 131104 | tf_op jit(solution)/shard_map/ppermute | solution.py:214
  22.1 2.2 %shard_map.115 = (bf16[1024,128]{1,0:T(8,128)(2,1)}, bf16[144,1024]{1,0:T(8,128)(2,1)S(1)}, bf16[1024,128]{1,0:T(8,128)(2,1)S(1)}, f32[8,64,128]{2,1,0:T(8,128)S(1)}, bf16[8,64,128]{2,1,0:T(8,128)(2,1)S(1)}) custom-call(f32[1,128]{1,0:T(1,128)S(1)} %bitcast.5, bf16[128,128]{1,0:T(8,128)(2,1)S(1)} %copy-done.1, bf16[1024,128]{1,0:T(8,128)(2,1)S(1)} %copy-done, ...), custom_call_target="tpu_custom_call" | custom-call | flops 67108864 | bytes 1048576 | tf_op jit(solution)/shard_map/pallas_call | solution.py:281
  24.4 1.7 %collective-permute-start.4 = (bf16[8,64,128]{2,1,0:T(8,128)(2,1)S(1)}, bf16[8,64,128]{2,1,0:T(8,128)(2,1)S(1)}, u32[]{:S(2)}, u32[]{:S(2)}) collective-permute-start(bf16[8,64,128]{2,1,0:T(8,128)(2,1)S(1)} %get-tuple-element.27), channel_id=1, source_target_pairs={{0,1},{1,0},{2,3},{3,2},{4,5},{5,4},{6,7},{7,6},{8,9},{9,8},{10,11... | collective-permute-start | bytes 393224 | tf_op jit(solution)/shard_map/ppermute | solution.py:214
  26.1 0.2 shard_map.117
  26.4 0.1 collective-permute-start.5
  26.4 1.2 %collective-permute-done.5 = f32[136,128]{1,0:T(8,128)S(1)} collective-permute-done((f32[136,128]{1,0:T(8,128)S(1)}, f32[136,128]{1,0:T(8,128)S(1)}, u32[]{:S(2)}, u32[]{:S(2)}) %collective-permute-start.5) | collective-permute-done | bytes 69664 | tf_op jit(solution)/shard_map/ppermute | solution.py:214
  27.7 1.7 %collective-permute-done.4.refs_1_ = bf16[8,64,128]{2,1,0:T(8,128)(2,1)S(1)} collective-permute-done((bf16[8,64,128]{2,1,0:T(8,128)(2,1)S(1)}, bf16[8,64,128]{2,1,0:T(8,128)(2,1)S(1)}, u32[]{:S(2)}, u32[]{:S(2)}) %collective-permute-start.4) | collective-permute-done | bytes 131104 | tf_op jit(solution)/shard_map/ppermute | solution.py:214
  29.5 2.0 %collective-permute-start.9 = (bf16[8,64,128]{2,1,0:T(8,128)(2,1)S(1)}, bf16[8,64,128]{2,1,0:T(8,128)(2,1)S(1)}, u32[]{:S(2)}, u32[]{:S(2)}) collective-permute-start(bf16[8,64,128]{2,1,0:T(8,128)(2,1)S(1)} %shard_map.116.g0), channel_id=1, source_target_pairs={{0,28},{2,30},{4,0},{6,2},{8,4},{10,6},{12,8},{14,10},{16,12},{18,... | collective-permute-start | bytes 393224 | tf_op jit(solution)/shard_map/ppermute | solution.py:214
  31.5 2.3 %collective-permute-done.6 = f32[136,128]{1,0:T(8,128)S(1)} collective-permute-done((f32[136,128]{1,0:T(8,128)S(1)}, f32[136,128]{1,0:T(8,128)S(1)}, u32[]{:S(2)}, u32[]{:S(2)}) %collective-permute-start.6) | collective-permute-done | bytes 69664 | tf_op jit(solution)/shard_map/ppermute | solution.py:214
  33.9 4.9 %collective-permute-done.7 = f32[136,128]{1,0:T(8,128)S(1)} collective-permute-done((f32[136,128]{1,0:T(8,128)S(1)}, f32[136,128]{1,0:T(8,128)S(1)}, u32[]{:S(2)}, u32[]{:S(2)}) %collective-permute-start.7) | collective-permute-done | bytes 69664 | tf_op jit(solution)/shard_map/ppermute | solution.py:214
  38.8 0.8 %collective-permute-start.8 = (f32[136,128]{1,0:T(8,128)S(1)}, f32[136,128]{1,0:T(8,128)S(1)}, u32[]{:S(2)}, u32[]{:S(2)}) collective-permute-start(f32[136,128]{1,0:T(8,128)S(1)} %add.14), channel_id=1, source_target_pairs={{0,16},{2,18},{4,20},{6,22},{8,24},{10,26},{12,28},{14,30},{16,0},... | collective-permute-start | bytes 208904 | tf_op jit(solution)/shard_map/ppermute | solution.py:214
  39.6 1.1 %shard_map.118.acc0 = f32[9,64,128]{2,1,0:T(8,128)S(1)} custom-call(s32[1]{0:T(128)S(6)} %copy.12.count, s32[96]{0:T(128)S(1)} %copy-done.2, s32[96]{0:T(128)S(1)} %copy-done.3, bf16[24,4,128,128]{3,2,1,0:T(8,128)(2,1)S(1)} %get-tuple-element.20.tiles, bf16[8,64,128]{2,1,0:T(8,128)(2,1)S(1)} %shard_map.116.g0), custom_call_target="tpu_custom_call" | custom-call | flops 50331648 | bytes 1048576 | tf_op jit(solution)/shard_map/pallas_call | solution.py:308
  40.8 1.2 %shard_map.119 = (f32[9,64,128]{2,1,0:T(8,128)S(1)}, f32[9,64,128]{2,1,0:T(8,128)S(1)}) custom-call(s32[1]{0:T(128)S(6)} %copy.12.count, s32[96]{0:T(128)S(1)} %copy-done.2, s32[96]{0:T(128)S(1)} %copy-done.3, bf16[24,4,128,128]{3,2,1,0:T(8,128)(2,1)S(1)} %get-tuple-element.20.tiles, bf16[8,64,128]{2,1,0:T(8,128)(2,1)S(1)} %collective-permute-done.9.g2, ...), custom_call_target="tpu_custom_call" | custom-call | flops 100663296 | bytes 1048576 | tf_op jit(solution)/shard_map/pallas_call | solution.py:310
  42.1 2.7 %collective-permute-done.8 = f32[136,128]{1,0:T(8,128)S(1)} collective-permute-done((f32[136,128]{1,0:T(8,128)S(1)}, f32[136,128]{1,0:T(8,128)S(1)}, u32[]{:S(2)}, u32[]{:S(2)}) %collective-permute-start.8) | collective-permute-done | bytes 69664 | tf_op jit(solution)/shard_map/ppermute | solution.py:214
  44.8 0.6 %slice.8 = f32[128,128]{1,0:T(8,128)} slice(f32[136,128]{1,0:T(8,128)S(1)} %add.15), slice={[0:128], [0:128]} | slice | bytes 131072 | tf_op jit(solution)/shard_map/slice | solution.py:323
  45.4 0.5 %slice_bitcast_fusion = f32[128]{0:T(128)} fusion(f32[136,128]{1,0:T(8,128)S(1)} %add.15), kind=kLoop, calls=%fused_computation | loop fusion | bytes 1024 | tf_op jit(solution)/shard_map/squeeze | solution.py:323
  45.9 1.8 %shard_map.120 = bf16[64,1024]{1,0:T(8,128)(2,1)} custom-call(s32[1]{0:T(128)S(6)} %copy.12.count, s32[96]{0:T(128)S(1)} %copy-done.2, s32[96]{0:T(128)S(1)} %copy-done.3, bf16[24,4,128,128]{3,2,1,0:T(8,128)(2,1)S(1)} %get-tuple-element.20.tiles, bf16[8,64,128]{2,1,0:T(8,128)(2,1)S(1)} %collective-permute-done.10.g, f32[9,64,128]{2,1,0:T(8,128)S(1)} %shard_map.118.acc0, ...), custom_call_target="tpu_custom_call" | custom-call | flops 50331648 | bytes 1048576 | tf_op jit(solution)/shard_map/pallas_call | solution.py:313
  (26 shorter events, 0.4 us)
Async XLA Ops:
  0.6 4.1 %copy-start.2 = (s32[96]{0:T(128)S(1)}, s32[96]{0:T(128)}, u32[]{:S(2)}) copy-start(s32[96]{0:T(128)} %src.7) | copy-start | bytes 1156
  0.6 4.0 %copy-start.3 = (s32[96]{0:T(128)S(1)}, s32[96]{0:T(128)}, u32[]{:S(2)}) copy-start(s32[96]{0:T(128)} %dst.7) | copy-start | bytes 1156
  1.3 20.8 %copy-start = (bf16[1024,128]{1,0:T(8,128)(2,1)S(1)}, bf16[1024,128]{1,0:T(8,128)(2,1)}, u32[]{:S(2)}) copy-start(bf16[1024,128]{1,0:T(8,128)(2,1)} %og_ref.1) | copy-start | bytes 786436
  1.3 20.8 %copy-start.1 = (bf16[128,128]{1,0:T(8,128)(2,1)S(1)}, bf16[128,128]{1,0:T(8,128)(2,1)}, u32[]{:S(2)}) copy-start(bf16[128,128]{1,0:T(8,128)(2,1)} %w_ref.1) | copy-start | bytes 98308
  1.3 20.8 %copy-start.4 = (f32[128]{0:T(128)S(1)}, f32[128]{0:T(128)}, u32[]{:S(2)}) copy-start(f32[128]{0:T(128)} %param.10) | copy-start | bytes 1540
  4.1 2.0 %collective-permute-start.1 = (bf16[8,64,128]{2,1,0:T(8,128)(2,1)S(1)}, bf16[8,64,128]{2,1,0:T(8,128)(2,1)S(1)}, u32[]{:S(2)}, u32[]{:S(2)}) collective-permute-start(bf16[8,64,128]{2,1,0:T(8,128)(2,1)S(1)} %get-tuple-element.24), channel_id=1, source_target_pairs={{0,2},{2,0},{4,6},{6,4},{8,10},{10,8},{12,14},{14,12},{16,18},{18,... | collective-permute-start | bytes 393224 | tf_op jit(solution)/shard_map/ppermute | solution.py:214
  4.6 7.4 %collective-permute-start = (bf16[8,64,128]{2,1,0:T(8,128)(2,1)S(1)}, bf16[8,64,128]{2,1,0:T(8,128)(2,1)S(1)}, u32[]{:S(2)}, u32[]{:S(2)}) collective-permute-start(bf16[8,64,128]{2,1,0:T(8,128)(2,1)S(1)} %get-tuple-element.22), channel_id=1, source_target_pairs={{0,2},{2,8},{4,6},{6,12},{8,10},{10,16},{12,14},{14,20},{16,18},{1... | collective-permute-start | bytes 393224 | tf_op jit(solution)/shard_map/ppermute | solution.py:214
  6.2 9.2 %collective-permute-start.2 = (bf16[8,64,128]{2,1,0:T(8,128)(2,1)S(1)}, bf16[8,64,128]{2,1,0:T(8,128)(2,1)S(1)}, u32[]{:S(2)}, u32[]{:S(2)}) collective-permute-start(bf16[8,64,128]{2,1,0:T(8,128)(2,1)S(1)} %shard_map.113), channel_id=1, source_target_pairs={{0,4},{2,6},{4,8},{6,10},{8,12},{10,14},{12,16},{14,18},{16,20},{1... | collective-permute-start | bytes 393224 | tf_op jit(solution)/shard_map/ppermute | solution.py:214
  15.4 6.7 %collective-permute-start.3 = (bf16[8,64,128]{2,1,0:T(8,128)(2,1)S(1)}, bf16[8,64,128]{2,1,0:T(8,128)(2,1)S(1)}, u32[]{:S(2)}, u32[]{:S(2)}) collective-permute-start(bf16[8,64,128]{2,1,0:T(8,128)(2,1)S(1)} %shard_map.114.refs_0_), channel_id=1, source_target_pairs={{0,1},{1,0},{2,3},{3,2},{4,5},{5,4},{6,7},{7,6},{8,9},{9,8},{10,11... | collective-permute-start | bytes 393224 | tf_op jit(solution)/shard_map/ppermute | solution.py:214
  24.4 5.0 %collective-permute-start.4 = (bf16[8,64,128]{2,1,0:T(8,128)(2,1)S(1)}, bf16[8,64,128]{2,1,0:T(8,128)(2,1)S(1)}, u32[]{:S(2)}, u32[]{:S(2)}) collective-permute-start(bf16[8,64,128]{2,1,0:T(8,128)(2,1)S(1)} %get-tuple-element.27), channel_id=1, source_target_pairs={{0,1},{1,0},{2,3},{3,2},{4,5},{5,4},{6,7},{7,6},{8,9},{9,8},{10,11... | collective-permute-start | bytes 393224 | tf_op jit(solution)/shard_map/ppermute | solution.py:214
  26.4 1.3 %collective-permute-start.5 = (f32[136,128]{1,0:T(8,128)S(1)}, f32[136,128]{1,0:T(8,128)S(1)}, u32[]{:S(2)}, u32[]{:S(2)}) collective-permute-start(f32[136,128]{1,0:T(8,128)S(1)} %shard_map.117), channel_id=1, source_target_pairs={{0,2},{2,0},{4,6},{6,4},{8,10},{10,8},{12,14},{14,12},{16,18},{18,... | collective-permute-start | bytes 208904 | tf_op jit(solution)/shard_map/ppermute | solution.py:214
  29.4 4.4 %collective-permute-start.6 = (f32[136,128]{1,0:T(8,128)S(1)}, f32[136,128]{1,0:T(8,128)S(1)}, u32[]{:S(2)}, u32[]{:S(2)}) collective-permute-start(f32[136,128]{1,0:T(8,128)S(1)} %add.12), channel_id=1, source_target_pairs={{0,4},{2,6},{4,0},{6,2},{8,12},{10,14},{12,8},{14,10},{16,20},{18,... | collective-permute-start | bytes 208904 | tf_op jit(solution)/shard_map/ppermute | solution.py:214
  29.5 11.3 %collective-permute-start.9 = (bf16[8,64,128]{2,1,0:T(8,128)(2,1)S(1)}, bf16[8,64,128]{2,1,0:T(8,128)(2,1)S(1)}, u32[]{:S(2)}, u32[]{:S(2)}) collective-permute-start(bf16[8,64,128]{2,1,0:T(8,128)(2,1)S(1)} %shard_map.116.g0), channel_id=1, source_target_pairs={{0,28},{2,30},{4,0},{6,2},{8,4},{10,6},{12,8},{14,10},{16,12},{18,... | collective-permute-start | bytes 393224 | tf_op jit(solution)/shard_map/ppermute | solution.py:214
  31.4 9.4 %collective-permute-start.11 = (bf16[8,64,128]{2,1,0:T(8,128)(2,1)S(1)}, bf16[8,64,128]{2,1,0:T(8,128)(2,1)S(1)}, u32[]{:S(2)}, u32[]{:S(2)}) collective-permute-start(bf16[8,64,128]{2,1,0:T(8,128)(2,1)S(1)} %shard_map.116.g0), channel_id=1, source_target_pairs={{0,26},{2,0},{4,30},{6,4},{8,2},{10,8},{12,6},{14,12},{16,10},{18,... | collective-permute-start | bytes 393224 | tf_op jit(solution)/shard_map/ppermute | solution.py:214
  33.8 5.0 %collective-permute-start.7 = (f32[136,128]{1,0:T(8,128)S(1)}, f32[136,128]{1,0:T(8,128)S(1)}, u32[]{:S(2)}, u32[]{:S(2)}) collective-permute-start(f32[136,128]{1,0:T(8,128)S(1)} %add.13), channel_id=1, source_target_pairs={{0,8},{2,10},{4,12},{6,14},{8,0},{10,2},{12,4},{14,6},{16,24},{18,... | collective-permute-start | bytes 208904 | tf_op jit(solution)/shard_map/ppermute | solution.py:214
  38.8 6.0 %collective-permute-start.8 = (f32[136,128]{1,0:T(8,128)S(1)}, f32[136,128]{1,0:T(8,128)S(1)}, u32[]{:S(2)}, u32[]{:S(2)}) collective-permute-start(f32[136,128]{1,0:T(8,128)S(1)} %add.14), channel_id=1, source_target_pairs={{0,16},{2,18},{4,20},{6,22},{8,24},{10,26},{12,28},{14,30},{16,0},... | collective-permute-start | bytes 208904 | tf_op jit(solution)/shard_map/ppermute | solution.py:214
  40.8 5.2 %collective-permute-start.10 = (bf16[8,64,128]{2,1,0:T(8,128)(2,1)S(1)}, bf16[8,64,128]{2,1,0:T(8,128)(2,1)S(1)}, u32[]{:S(2)}, u32[]{:S(2)}) collective-permute-start(bf16[8,64,128]{2,1,0:T(8,128)(2,1)S(1)} %collective-permute-done.9.g2), channel_id=1, source_target_pairs={{0,2},{2,0},{4,6},{6,4},{8,10},{10,8},{12,14},{14,12},{16,18},{18,... | collective-permute-start | bytes 393224 | tf_op jit(solution)/shard_map/ppermute | solution.py:214
where the time goes:
time: 47.9 us; the launch traced here: 47.8 us
  waiting for transfers between devices  22.9 us (48%)
  starting transfers between devices  11.3 us (24%)
  Pallas kernels  10.9 us (23%)
  between operations  1.47 us (3%)
  local copies, waits for them, and re-layouts  1.17 us (2%)
    ppermute x12, waiting for transfers between devices, moved(): return lax.ppermute(block, axis, [(i, target(i) % n) for i in range(n)])  22.9 us
    ppermute x12, starting transfers between devices, moved(): return lax.ppermute(block, axis, [(i, target(i) % n) for i in range(n)])  11.3 us
    pallas_call x1, Pallas kernels, shards(): call(forward_far_kernel, [tiles, piece, piece, piece], [SMEM] + [HBM] * 4...  2.75 us
    pallas_call x1, Pallas kernels, shards(): call(functools.partial(middle_kernel, parts), [jax.ShapeDtypeStruct((node...  2.25 us
    pallas_call x1, Pallas kernels, shards(): call(backward_last_kernel, [jax.ShapeDtypeStruct((width, nodes), BF16)],...  1.84 us
    pallas_call x1, Pallas kernels, shards(): call(forward_near_kernel, [totals, totals], [SMEM] * 3 + [VMEM] * 2, (),...  1.44 us
    pallas_call x1, Pallas kernels, shards(): call(backward_near_kernel, [totals, totals], [SMEM] * 3 + [VMEM] * 3, (),...  1.25 us
    pallas_call x1, Pallas kernels, shards(): call(backward_own_kernel, [totals], [SMEM] * 3 + [VMEM] * 2, (), flops)  1.11 us
  transfers between devices with their start and end apart: 12, of which 8 were waited for; matrix products, arithmetic and copies ran while one was open for 2% of the time, Pallas kernels for 8%

commit v1 on v0

v1 whole, which is shorter than its diff:
```python
import functools

import jax
import jax.numpy as jnp
from jax import lax
from jax.experimental import pallas as pl
from jax.experimental.pallas import tpu as pltpu
from jax.sharding import PartitionSpec as P

BLOCK = 128
REACH = 4
F32 = jnp.float32
BF16 = jnp.bfloat16
VMEM = pl.BlockSpec(memory_space=pltpu.VMEM)
SMEM = pl.BlockSpec(memory_space=pltpu.SMEM)
HBM = pl.BlockSpec(memory_space=pltpu.HBM)


def call(kernel, out_shape, in_specs, out_specs, scratch=(), flops=0):
    return pl.pallas_call(
        kernel,
        out_shape=out_shape,
        in_specs=in_specs,
        out_specs=out_specs,
        scratch_shapes=list(scratch),
        compiler_params=pltpu.CompilerParams(vmem_limit_bytes=24 * 1024 * 1024),
        cost_estimate=pl.CostEstimate(flops=flops, bytes_accessed=2**20, transcendentals=0),
    )


def groups_at_once(groups):
    return next(m for m in (4, 3, 2, 1) if groups % m == 0)


def in_hbm(a):
    return pltpu.with_memory_space_constraint(a, pltpu.HBM)


def own_core():
    return lax.rem(lax.axis_index("dom"), 2)


def slot_loop(count, groups, offsets, body, arrive=None):
    m = groups_at_once(groups)

    def chunk(i, carry):
        if arrive is not None:
            arrive(i)

        @pl.when(i * (m * REACH) < count)
        def _():
            for u in range(m):
                for o in offsets:
                    j = i * m + u
                    body(j, o, j * REACH + o < count)

        return carry

    lax.fori_loop(0, groups // m, chunk, 0)


def push(xt, tiles_ref, src_ref, dst_ref, acc, j, o, live):
    blocks = xt.shape[0]
    k = j * REACH + o
    d = jnp.where(live, dst_ref[k] - o * blocks, blocks)
    acc[d] += lax.dot_general(
        xt[src_ref[k]], tiles_ref[j, o], (((1,), (1,)), ((), ())), preferred_element_type=F32
    )


def forward_swap_kernel(
    count, src_hbm, dst_hbm, x_hbm, tiles_hbm, tiles, xt, swap, src, dst, x, acc, small, large
):
    blocks, width, _ = xt.shape
    groups = tiles.shape[0]
    m = groups_at_once(groups)
    copies = [
        pltpu.make_async_copy(a, b, small.at[i])
        for i, (a, b) in enumerate(((x_hbm, x), (src_hbm, src), (dst_hbm, dst)))
    ]

    def chunk(i):
        part = pl.ds(i * m, m)
        return pltpu.make_async_copy(tiles_hbm.at[part], tiles.at[part], large.at[i])

    for c in copies:
        c.start()
    for i in range(groups // m):
        chunk(i).start()
    acc[...] = jnp.zeros_like(acc)
    row = lax.broadcasted_iota(jnp.int32, (width, x.shape[1]), 0)
    column = lax.broadcasted_iota(jnp.int32, (width, x.shape[1]), 1)
    pick = (column == row + lax.axis_index("feat") * width).astype(BF16)
    for c in copies:
        c.wait()
    for b in range(blocks):
        xt[b] = lax.dot_general(
            pick, x[b * BLOCK : (b + 1) * BLOCK, :], (((1,), (1,)), ((), ())), preferred_element_type=F32
        ).astype(BF16)
    o = 3 - 2 * own_core()
    slot_loop(
        count[0], groups, (o,), functools.partial(push, xt, tiles, src, dst, acc), lambda i: chunk(i).wait()
    )
    swap[...] = acc[:blocks].astype(BF16)


def forward_send_kernel(count, src, dst, xt, tiles, acc2, direct, acc):
    acc2[...] = jnp.zeros_like(acc2)
    acc[...] = jnp.zeros_like(acc)
    far = 1 + 2 * own_core()

    def body(j, o, live):
        push(xt, tiles, src, dst, acc2 if isinstance(o, int) else acc, j, o, live)

    slot_loop(count[0], tiles.shape[0], (2, far), body)
    direct[...] = acc[: direct.shape[0]].astype(BF16)


def forward_own_kernel(count, src, dst, xt, tiles, acc):
    acc[...] = jnp.zeros_like(acc)
    slot_loop(count[0], tiles.shape[0], (0,), functools.partial(push, xt, tiles, src, dst, acc))


def sum_kernel(n, *refs):
    out = refs[n]
    blocks = out.shape[0]
    total = refs[0][:blocks].astype(F32)
    for r in refs[1:n]:
        total = total + r[:blocks].astype(F32)
    out[...] = total.astype(out.dtype)


def middle_kernel(parts, bias_ref, w_ref, og_ref, *refs):
    h_refs, (out_ref, ht, grads), g_refs = refs[:parts], refs[parts : parts + 3], refs[parts + 3 :]
    blocks, width, _ = h_refs[0].shape
    f_in = w_ref.shape[0]
    me = lax.axis_index("feat")
    for q in range(parts):
        row = pl.multiple_of(lax.rem(me + q, parts) * width, width)
        for b in range(blocks):
            ht[pl.ds(row, width), b * BLOCK : (b + 1) * BLOCK] = h_refs[q][b]
    ht[f_in:, :] = jnp.ones((ht.shape[0] - f_in, ht.shape[1]), BF16)
    for b in range(blocks):
        rows = slice(b * BLOCK, (b + 1) * BLOCK)
        pre = lax.dot_general(
            ht[:f_in, rows], w_ref[...], (((0,), (0,)), ((), ())), preferred_element_type=F32
        ) + bias_ref[...]
        s = jax.nn.sigmoid(pre)
        out_ref[rows, :] = (pre * s).astype(BF16)
        grad = (og_ref[rows, :].astype(F32) * s * (1.0 + pre * (1.0 - s))).astype(BF16)
        grads[rows, :] = grad
        for q in range(parts):
            row = pl.multiple_of(lax.rem(me + q, parts) * width, width)
            g_refs[q][b] = lax.dot_general(
                w_ref[pl.ds(row, width), :], grad, (((1,), (1,)), ((), ())), preferred_element_type=F32
            ).astype(g_refs[q].dtype)


def weight_grad_kernel(ht, grads, act, out, wg, sem):
    copy = pltpu.make_async_copy(act, out, sem)
    copy.start()
    full = jnp.dot(ht[...], grads[...], preferred_element_type=F32)
    wg[...] = full[: wg.shape[0]]
    copy.wait()


def pull(g, tiles, src, dst, acc, j, o, live):
    blocks = g.shape[0]
    k = j * REACH + o
    s = jnp.where(live, src[k], blocks)
    acc[s] += jnp.dot(g[dst[k] - o * blocks], tiles[j, o], preferred_element_type=F32)


def backward_own_kernel(count, src, dst, tiles, g0, acc):
    acc[...] = jnp.zeros_like(acc)
    slot_loop(count[0], tiles.shape[0], (0,), functools.partial(pull, g0, tiles, src, dst, acc))


def backward_near_kernel(count, src, dst, tiles, g2, gd, acc2, accd):
    acc2[...] = jnp.zeros_like(acc2)
    accd[...] = jnp.zeros_like(accd)
    far = 1 + 2 * own_core()

    def body(j, o, live):
        if isinstance(o, int):
            pull(g2, tiles, src, dst, acc2, j, o, live)
        else:
            pull(gd, tiles, src, dst, accd, j, o, live)

    slot_loop(count[0], tiles.shape[0], (2, far), body)


def backward_last_kernel(count, src, dst, tiles, g, acc0, acc2, accd, *refs):
    parts, (out, wg, bias, acc) = refs[:-4], refs[-4:]
    blocks = g.shape[0]
    acc[...] = jnp.zeros_like(acc)
    far = 3 - 2 * own_core()
    slot_loop(count[0], tiles.shape[0], (far,), functools.partial(pull, g, tiles, src, dst, acc))
    for b in range(blocks):
        total = acc[b] + acc0[b] + acc2[b] + accd[b]
        out[:, b * BLOCK : (b + 1) * BLOCK] = total.astype(BF16)
    whole = paired_sum([r[...] for r in parts])
    f_in = wg.shape[0]
    wg[...] = whole[:f_in]
    bias[...] = whole[f_in : f_in + 1]


def paired_sum(parts):
    if len(parts) == 4:
        return (parts[0] + parts[2]) + (parts[1] + parts[3])
    return functools.reduce(lambda a, b: a + b, parts)


def paired_sum_kernel(*refs):
    refs[-1][...] = paired_sum([r[...] for r in refs[:-1]])


def moved(block, axis, target):
    n = lax.axis_size(axis)
    return lax.ppermute(block, axis, [(i, target(i) % n) for i in range(n)])


def radices(n):
    out = []
    while n > 1:
        r = 4 if n % 4 == 0 else 2 if n % 2 == 0 else n
        out.append(r)
        n //= r
    return out


def exchanged(part, axis, stride, r):
    def target(step, i):
        digit = i // stride % r
        return i + ((digit + step) % r - digit) * stride

    return [part] + [moved(part, axis, functools.partial(target, s)) for s in range(1, r)]


def shards(node_features, weight, bias, tile_values, tile_src, tile_dst, tile_counts, out_grad):
    nodes, f_in = node_features.shape
    hid = weight.shape[1]
    blocks = nodes // BLOCK
    parts = lax.axis_size("feat")
    width = f_in // parts
    capacity = tile_values.shape[0]
    groups = capacity // REACH
    piece = jax.ShapeDtypeStruct((blocks, width, BLOCK), BF16)
    wide = jax.ShapeDtypeStruct((blocks, width, BLOCK), F32)
    totals = jax.ShapeDtypeStruct((blocks + 1, width, BLOCK), F32)
    acc = pltpu.VMEM(totals.shape, F32)
    tiles = jax.ShapeDtypeStruct((groups, REACH, BLOCK, BLOCK), BF16)
    slots = jax.ShapeDtypeStruct((capacity,), jnp.int32)
    rows = jax.ShapeDtypeStruct((nodes, hid), BF16)
    gradient = jax.ShapeDtypeStruct((f_in + 8, hid), F32)
    m = groups_at_once(groups)
    flops = 2 * capacity * BLOCK * BLOCK * width // REACH

    def swapped(i):
        return i ^ 1

    tiles, xt, swap, src, dst = call(
        forward_swap_kernel,
        [tiles, piece, piece, slots, slots],
        [SMEM] + [HBM] * 4,
        [VMEM] * 3 + [SMEM] * 2,
        [
            pltpu.VMEM(node_features.shape, BF16),
            acc,
            pltpu.SemaphoreType.DMA((3,)),
            pltpu.SemaphoreType.DMA((groups // m,)),
        ],
        flops,
    )(tile_counts, *(in_hbm(a) for a in (tile_src, tile_dst, node_features, tile_values.reshape(tiles.shape))))
    index = (tile_counts, src, dst)
    swap = moved(swap, "dom", swapped)
    acc2, direct = call(
        forward_send_kernel, [totals, piece], [SMEM] * 3 + [VMEM] * 2, [VMEM] * 2, [acc], 2 * flops
    )(*index, xt, tiles)
    (chip,) = call(functools.partial(sum_kernel, 2), [piece], [VMEM] * 2, [VMEM])(acc2, swap)
    chip = moved(chip, "dom", lambda i: i + 2)
    direct = moved(direct, "dom", lambda i: i + 1 + 2 * (i % 2))
    (acc0,) = call(forward_own_kernel, [totals], [SMEM] * 3 + [VMEM] * 2, [VMEM], (), flops)(*index, xt, tiles)
    (h,) = call(functools.partial(sum_kernel, 3), [piece], [VMEM] * 3, [VMEM])(acc0, direct, chip)
    hs = [h] + [moved(h, "feat", lambda i, q=q: i - q) for q in range(1, parts)]
    act, ht, grads, g_own, *g_others = call(
        functools.partial(middle_kernel, parts),
        [rows, jax.ShapeDtypeStruct((f_in + 16, nodes), BF16), rows, wide] + [piece] * (parts - 1),
        [VMEM] * (3 + parts),
        [VMEM] * (3 + parts),
        (),
        4 * nodes * f_in * hid,
    )(bias.reshape(1, hid), weight, out_grad, *hs)
    g_received = [moved(g, "feat", lambda i, q=q + 1: i + q) for q, g in enumerate(g_others)]
    output, wg = call(
        weight_grad_kernel,
        [rows, gradient],
        [VMEM] * 3,
        [HBM, VMEM],
        [pltpu.SemaphoreType.DMA],
        2 * nodes * f_in * hid,
    )(ht, grads, act)
    g_own, wg = lax.optimization_barrier((g_own, wg))
    (g,) = call(functools.partial(sum_kernel, parts), [piece], [VMEM] * parts, [VMEM])(g_own, *g_received)
    g_chip = moved(g, "dom", lambda i: i - 2)
    g_direct = moved(g, "dom", lambda i: i - 3 + 2 * (i % 2))
    wgs, stride = [wg], 1
    for r in radices(lax.axis_size("dom")):
        if len(wgs) > 1:
            (wg,) = call(paired_sum_kernel, [gradient], [VMEM] * len(wgs), [VMEM])(*wgs)
        wgs = exchanged(wg, "dom", stride, r)
        stride *= r
    (back0,) = call(backward_own_kernel, [totals], [SMEM] * 3 + [VMEM] * 2, [VMEM], (), flops)(*index, tiles, g)
    g_swap = moved(g_chip, "dom", swapped)
    back2, backd = call(
        backward_near_kernel, [totals, totals], [SMEM] * 3 + [VMEM] * 3, [VMEM] * 2, (), 2 * flops
    )(*index, tiles, g_chip, g_direct)
    input_grad, weight_grad, bias_grad = call(
        backward_last_kernel,
        [
            jax.ShapeDtypeStruct((width, nodes), BF16),
            jax.ShapeDtypeStruct((f_in, hid), F32),
            jax.ShapeDtypeStruct((1, hid), F32),
        ],
        [SMEM] * 3 + [VMEM] * (5 + len(wgs)),
        [VMEM] * 3,
        [acc],
        flops,
    )(*index, tiles, g_swap, back0, back2, backd, *wgs)
    return output, weight_grad, bias_grad.reshape(hid), input_grad.T


def solution(mesh):
    return jax.shard_map(
        shards,
        mesh=mesh,
        in_specs=(
            P("dom", None),
            P(None, "feat"),
            P("feat"),
            P("dom", None, None),
            P("dom"),
            P("dom"),
            P("dom"),
            P("dom", "feat"),
        ),
        out_specs=(P("dom", "feat"), P(None, "feat"), P("feat"), P("dom", "feat")),
        check_vma=False,
    )
```

time: 47.9 us -> 48.5 us (1.013)
  starting transfers between devices: 11.3 us -> 14.4 us
  waiting for transfers between devices: 22.9 us -> 20.1 us
  Pallas kernels: 10.9 us -> 12.5 us
  local copies, waits for them, and re-layouts: 1.17 us -> 0.02 us
    ppermute x12 -> x14, starting transfers between devices: 11.3 us -> 14.4 us  [moved(): return lax.ppermute(block, axis, [(i, target(i) % n) for i in range(n)])]
    ppermute x12 -> x14, waiting for transfers between devices: 22.9 us -> 20.1 us  [moved(): return lax.ppermute(block, axis, [(i, target(i) % n) for i in range(n)])]
    pallas_call x10 -> x12, Pallas kernels: 10.9 us -> 12.5 us  [the longest x1 3.05 us: shards(): call(forward_swap_kernel, [tiles, piece, piece, slots, slots], [SMEM] + [...]
    slice x1 -> x0, local copies, waits for them, and re-layouts: 0.63 us -> none  [shards(): return (output, wg[:f_in], wg[f_in], input_grad.T)]
    squeeze x1 -> x0, local copies, waits for them, and re-layouts: 0.51 us -> none  [shards(): return (output, wg[:f_in], wg[f_in], input_grad.T)]
  transfers between devices with their start and end apart: 12 -> 14, of which waited for: 8 -> 8; matrix products, arithmetic and copies ran while one was open for 2% -> 0% of each run, Pallas kernels for 8% -> 12%
where the time goes in v1:
time: 48.5 us; the launch traced here: 48.4 us
  waiting for transfers between devices  20.1 us (41%)
  starting transfers between devices  14.4 us (30%)
  Pallas kernels  12.5 us (26%)
  between operations  1.4 us (3%)
    ppermute x14, waiting for transfers between devices, moved(): return lax.ppermute(block, axis, [(i, target(i) % n) for i in range(n)])  20.1 us
    ppermute x14, starting transfers between devices, moved(): return lax.ppermute(block, axis, [(i, target(i) % n) for i in range(n)])  14.4 us
    pallas_call x1, Pallas kernels, shards(): call(forward_swap_kernel, [tiles, piece, piece, slots, slots], [SMEM] + [...  3.05 us
    pallas_call x1, Pallas kernels, shards(): call(backward_last_kernel, [jax.ShapeDtypeStruct((width, nodes), BF16), j...  1.88 us
    pallas_call x1, Pallas kernels, shards(): call(functools.partial(middle_kernel, parts), [rows, jax.ShapeDtypeStruct...  1.67 us
    pallas_call x1, Pallas kernels, shards(): call(forward_send_kernel, [totals, piece], [SMEM] * 3 + [VMEM] * 2, [VMEM...  1.47 us
    pallas_call x1, Pallas kernels, shards(): call(backward_near_kernel, [totals, totals], [SMEM] * 3 + [VMEM] * 3, [VM...  1.23 us
    pallas_call x1, Pallas kernels, shards(): call(forward_own_kernel, [totals], [SMEM] * 3 + [VMEM] * 2, [VMEM], (), f...  1.21 us
  transfers between devices with their start and end apart: 14, of which 8 were waited for; matrix products, arithmetic and copies ran while one was open for 0% of the time, Pallas kernels for 12%

profile of v1, /device:TPU:0, one launch (start us, length us, event | category | flops | bytes accessed | tf_op | source)
XLA Modules:
  0.0 48.4 jit_solution(2679168096906559076)
XLA Ops:
  1.3 3.1 %shard_map.111 = (bf16[24,4,128,128]{3,2,1,0:T(8,128)(2,1)S(1)}, bf16[8,64,128]{2,1,0:T(8,128)(2,1)S(1)}, bf16[8,64,128]{2,1,0:T(8,128)(2,1)S(1)}, s32[96]{0:T(128)S(1)}, s32[96]{0:T(128)S(1)}) custom-call(s32[1]{0:T(128)S(6)} %copy.12.count, s32[96]{0:T(128)} %src_hbm.1, s32[96]{0:T(128)} %dst_hbm.1, bf16[1024,128]{1,0:T(8,128)(2,1)} %x_hbm.1, ...), custom_call_target="tpu_custom_call" | custom-call | flops 50331648 | bytes 1048576 | tf_op jit(solution)/shard_map/pallas_call | solution.py:262
  4.9 1.5 %shard_map.113 = (f32[9,64,128]{2,1,0:T(8,128)S(1)}, bf16[8,64,128]{2,1,0:T(8,128)(2,1)S(1)}) custom-call(s32[1]{0:T(128)S(6)} %copy.12.count, s32[96]{0:T(128)S(1)} %get-tuple-element.25.src, s32[96]{0:T(128)S(1)} %get-tuple-element.26.dst, bf16[8,64,128]{2,1,0:T(8,128)(2,1)S(1)} %get-tuple-element.27.xt, bf16[24,4,128,128]{3,2,1,0:T(8,128)(2,1)S(1)} %get-tuple-element.28.tiles), custom_call_target="tpu_custom_call" | custom-call | flops 100663296 | bytes 1048576 | tf_op jit(solution)/shard_map/pallas_call | solution.py:277
  6.5 2.7 %collective-permute-start.2 = (bf16[8,64,128]{2,1,0:T(8,128)(2,1)S(1)}, bf16[8,64,128]{2,1,0:T(8,128)(2,1)S(1)}, u32[]{:S(2)}, u32[]{:S(2)}) collective-permute-start(bf16[8,64,128]{2,1,0:T(8,128)(2,1)S(1)} %shard_map.114), channel_id=1, source_target_pairs={{0,4},{2,6},{4,8},{6,10},{8,12},{10,14},{12,16},{14,18},{16,20},{1... | collective-permute-start | bytes 393224 | tf_op jit(solution)/shard_map/ppermute | solution.py:220
  9.3 1.2 %shard_map.112.refs_0_ = f32[9,64,128]{2,1,0:T(8,128)S(1)} custom-call(s32[1]{0:T(128)S(6)} %copy.12.count, s32[96]{0:T(128)S(1)} %get-tuple-element.25.src, s32[96]{0:T(128)S(1)} %get-tuple-element.26.dst, bf16[8,64,128]{2,1,0:T(8,128)(2,1)S(1)} %get-tuple-element.27.xt, bf16[24,4,128,128]{3,2,1,0:T(8,128)(2,1)S(1)} %get-tuple-element.28.tiles), custom_call_target="tpu_custom_call" | custom-call | flops 50331648 | bytes 1048576 | tf_op jit(solution)/shard_map/pallas_call | solution.py:283
  10.5 3.1 %collective-permute-done.refs_1_ = bf16[8,64,128]{2,1,0:T(8,128)(2,1)S(1)} collective-permute-done((bf16[8,64,128]{2,1,0:T(8,128)(2,1)S(1)}, bf16[8,64,128]{2,1,0:T(8,128)(2,1)S(1)}, u32[]{:S(2)}, u32[]{:S(2)}) %collective-permute-start) | collective-permute-done | bytes 131104 | tf_op jit(solution)/shard_map/ppermute | solution.py:220
  13.6 4.3 %collective-permute-done.2.refs_2_ = bf16[8,64,128]{2,1,0:T(8,128)(2,1)S(1)} collective-permute-done((bf16[8,64,128]{2,1,0:T(8,128)(2,1)S(1)}, bf16[8,64,128]{2,1,0:T(8,128)(2,1)S(1)}, u32[]{:S(2)}, u32[]{:S(2)}) %collective-permute-start.2) | collective-permute-done | bytes 131104 | tf_op jit(solution)/shard_map/ppermute | solution.py:220
  17.9 1.6 %collective-permute-start.3 = (bf16[8,64,128]{2,1,0:T(8,128)(2,1)S(1)}, bf16[8,64,128]{2,1,0:T(8,128)(2,1)S(1)}, u32[]{:S(2)}, u32[]{:S(2)}) collective-permute-start(bf16[8,64,128]{2,1,0:T(8,128)(2,1)S(1)} %shard_map.115.refs_0_), channel_id=1, source_target_pairs={{0,1},{1,0},{2,3},{3,2},{4,5},{5,4},{6,7},{7,6},{8,9},{9,8},{10,11... | collective-permute-start | bytes 393224 | tf_op jit(solution)/shard_map/ppermute | solution.py:220
  19.5 4.0 %collective-permute-done.3.refs_1_ = bf16[8,64,128]{2,1,0:T(8,128)(2,1)S(1)} collective-permute-done((bf16[8,64,128]{2,1,0:T(8,128)(2,1)S(1)}, bf16[8,64,128]{2,1,0:T(8,128)(2,1)S(1)}, u32[]{:S(2)}, u32[]{:S(2)}) %collective-permute-start.3) | collective-permute-done | bytes 131104 | tf_op jit(solution)/shard_map/ppermute | solution.py:220
  23.5 1.7 %shard_map.116 = (bf16[1024,128]{1,0:T(8,128)(2,1)S(1)}, bf16[144,1024]{1,0:T(8,128)(2,1)S(1)}, bf16[1024,128]{1,0:T(8,128)(2,1)S(1)}, f32[8,64,128]{2,1,0:T(8,128)S(1)}, bf16[8,64,128]{2,1,0:T(8,128)(2,1)S(1)}) custom-call(f32[1,128]{1,0:T(1,128)S(1)} %bitcast.4, bf16[128,128]{1,0:T(8,128)(2,1)S(1)} %copy-done.1, bf16[1024,128]{1,0:T(8,128)(2,1)S(1)} %copy-done, ...), custom_call_target="tpu_custom_call" | custom-call | flops 67108864 | bytes 1048576 | tf_op jit(solution)/shard_map/pallas_call | solution.py:286
  25.2 1.5 %collective-permute-start.4 = (bf16[8,64,128]{2,1,0:T(8,128)(2,1)S(1)}, bf16[8,64,128]{2,1,0:T(8,128)(2,1)S(1)}, u32[]{:S(2)}, u32[]{:S(2)}) collective-permute-start(bf16[8,64,128]{2,1,0:T(8,128)(2,1)S(1)} %get-tuple-element.39), channel_id=1, source_target_pairs={{0,1},{1,0},{2,3},{3,2},{4,5},{5,4},{6,7},{7,6},{8,9},{9,8},{10,11... | collective-permute-start | bytes 393224 | tf_op jit(solution)/shard_map/ppermute | solution.py:220
  26.7 0.7 %shard_map.117 = (bf16[1024,128]{1,0:T(8,128)(2,1)}, f32[136,128]{1,0:T(8,128)S(1)}) custom-call(bf16[144,1024]{1,0:T(8,128)(2,1)S(1)} %get-tuple-element.32.ht, bf16[1024,128]{1,0:T(8,128)(2,1)S(1)} %get-tuple-element.33.grads, bf16[1024,128]{1,0:T(8,128)(2,1)S(1)} %get-tuple-element.34.act), custom_call_target="tpu_custom_call" | custom-call | flops 33554432 | bytes 1048576 | tf_op jit(solution)/shard_map/pallas_call | solution.py:295
  27.5 2.7 %collective-permute-done.4.refs_1_ = bf16[8,64,128]{2,1,0:T(8,128)(2,1)S(1)} collective-permute-done((bf16[8,64,128]{2,1,0:T(8,128)(2,1)S(1)}, bf16[8,64,128]{2,1,0:T(8,128)(2,1)S(1)}, u32[]{:S(2)}, u32[]{:S(2)}) %collective-permute-start.4) | collective-permute-done | bytes 131104 | tf_op jit(solution)/shard_map/ppermute | solution.py:220
  30.5 0.6 %collective-permute-start.7 = (bf16[8,64,128]{2,1,0:T(8,128)(2,1)S(1)}, bf16[8,64,128]{2,1,0:T(8,128)(2,1)S(1)}, u32[]{:S(2)}, u32[]{:S(2)}) collective-permute-start(bf16[8,64,128]{2,1,0:T(8,128)(2,1)S(1)} %shard_map.118.g0), channel_id=1, source_target_pairs={{0,26},{2,0},{4,30},{6,4},{8,2},{10,8},{12,6},{14,12},{16,10},{18,... | collective-permute-start | bytes 393224 | tf_op jit(solution)/shard_map/ppermute | solution.py:220
  31.1 1.7 %collective-permute-start.9 = (f32[136,128]{1,0:T(8,128)S(1)}, f32[136,128]{1,0:T(8,128)S(1)}, u32[]{:S(2)}, u32[]{:S(2)}) collective-permute-start(f32[136,128]{1,0:T(8,128)S(1)} %get-tuple-element.42.refs_0_), channel_id=1, source_target_pairs={{0,4},{2,6},{4,0},{6,2},{8,12},{10,14},{12,8},{14,10},{16,20},{18,... | collective-permute-start | bytes 208904 | tf_op jit(solution)/shard_map/ppermute | solution.py:220
  32.8 1.4 %collective-permute-start.10 = (f32[136,128]{1,0:T(8,128)S(1)}, f32[136,128]{1,0:T(8,128)S(1)}, u32[]{:S(2)}, u32[]{:S(2)}) collective-permute-start(f32[136,128]{1,0:T(8,128)S(1)} %get-tuple-element.42.refs_0_), channel_id=1, source_target_pairs={{0,6},{2,0},{4,2},{6,4},{8,14},{10,8},{12,10},{14,12},{16,22},{18,... | collective-permute-start | bytes 208904 | tf_op jit(solution)/shard_map/ppermute | solution.py:220
  34.3 2.1 %collective-permute-done.5.g2 = bf16[8,64,128]{2,1,0:T(8,128)(2,1)S(1)} collective-permute-done((bf16[8,64,128]{2,1,0:T(8,128)(2,1)S(1)}, bf16[8,64,128]{2,1,0:T(8,128)(2,1)S(1)}, u32[]{:S(2)}, u32[]{:S(2)}) %collective-permute-start.5) | collective-permute-done | bytes 131104 | tf_op jit(solution)/shard_map/ppermute | solution.py:220
  36.4 1.1 %collective-permute-done.9.refs_2_ = f32[136,128]{1,0:T(8,128)S(1)} collective-permute-done((f32[136,128]{1,0:T(8,128)S(1)}, f32[136,128]{1,0:T(8,128)S(1)}, u32[]{:S(2)}, u32[]{:S(2)}) %collective-permute-start.9) | collective-permute-done | bytes 69664 | tf_op jit(solution)/shard_map/ppermute | solution.py:220
  37.6 2.2 %collective-permute-start.12 = (f32[136,128]{1,0:T(8,128)S(1)}, f32[136,128]{1,0:T(8,128)S(1)}, u32[]{:S(2)}, u32[]{:S(2)}) collective-permute-start(f32[136,128]{1,0:T(8,128)S(1)} %shard_map.121.refs_0_), channel_id=1, source_target_pairs={{0,16},{2,18},{4,20},{6,22},{8,24},{10,26},{12,28},{14,30},{16,0},... | collective-permute-start | bytes 208904 | tf_op jit(solution)/shard_map/ppermute | solution.py:220
  39.7 1.7 %collective-permute-start.13 = (f32[136,128]{1,0:T(8,128)S(1)}, f32[136,128]{1,0:T(8,128)S(1)}, u32[]{:S(2)}, u32[]{:S(2)}) collective-permute-start(f32[136,128]{1,0:T(8,128)S(1)} %shard_map.121.refs_0_), channel_id=1, source_target_pairs={{0,24},{2,26},{4,28},{6,30},{8,0},{10,2},{12,4},{14,6},{16,8},{18,... | collective-permute-start | bytes 208904 | tf_op jit(solution)/shard_map/ppermute | solution.py:220
  41.4 1.1 %shard_map.119.acc0 = f32[9,64,128]{2,1,0:T(8,128)S(1)} custom-call(s32[1]{0:T(128)S(6)} %copy.12.count, s32[96]{0:T(128)S(1)} %get-tuple-element.25.src, s32[96]{0:T(128)S(1)} %get-tuple-element.26.dst, bf16[24,4,128,128]{3,2,1,0:T(8,128)(2,1)S(1)} %get-tuple-element.28.tiles, bf16[8,64,128]{2,1,0:T(8,128)(2,1)S(1)} %shard_map.118.g0), custom_call_target="tpu_custom_call" | custom-call | flops 50331648 | bytes 1048576 | tf_op jit(solution)/shard_map/pallas_call | solution.py:313
  42.5 1.2 %shard_map.120 = (f32[9,64,128]{2,1,0:T(8,128)S(1)}, f32[9,64,128]{2,1,0:T(8,128)S(1)}) custom-call(s32[1]{0:T(128)S(6)} %copy.12.count, s32[96]{0:T(128)S(1)} %get-tuple-element.25.src, s32[96]{0:T(128)S(1)} %get-tuple-element.26.dst, bf16[24,4,128,128]{3,2,1,0:T(8,128)(2,1)S(1)} %get-tuple-element.28.tiles, ...), custom_call_target="tpu_custom_call" | custom-call | flops 100663296 | bytes 1048576 | tf_op jit(solution)/shard_map/pallas_call | solution.py:315
  43.8 0.7 %collective-permute-done.11.refs_1_ = f32[136,128]{1,0:T(8,128)S(1)} collective-permute-done((f32[136,128]{1,0:T(8,128)S(1)}, f32[136,128]{1,0:T(8,128)S(1)}, u32[]{:S(2)}, u32[]{:S(2)}) %collective-permute-start.11) | collective-permute-done | bytes 69664 | tf_op jit(solution)/shard_map/ppermute | solution.py:220
  44.4 2.1 %collective-permute-done.12.refs_2_ = f32[136,128]{1,0:T(8,128)S(1)} collective-permute-done((f32[136,128]{1,0:T(8,128)S(1)}, f32[136,128]{1,0:T(8,128)S(1)}, u32[]{:S(2)}, u32[]{:S(2)}) %collective-permute-start.12) | collective-permute-done | bytes 69664 | tf_op jit(solution)/shard_map/ppermute | solution.py:220
  46.5 1.9 %shard_map.122 = (bf16[64,1024]{1,0:T(8,128)(2,1)}, f32[128,128]{1,0:T(8,128)}, f32[1,128]{1,0:T(1,128)}) custom-call(s32[1]{0:T(128)S(6)} %copy.12.count, s32[96]{0:T(128)S(1)} %get-tuple-element.25.src, s32[96]{0:T(128)S(1)} %get-tuple-element.26.dst, bf16[24,4,128,128]{3,2,1,0:T(8,128)(2,1)S(1)} %get-tuple-element.28.tiles, ...), custom_call_target="tpu_custom_call" | custom-call | flops 50331648 | bytes 1048576 | tf_op jit(solution)/shard_map/pallas_call | solution.py:318
  (22 shorter events, 1.2 us)
Async XLA Ops:
  4.3 2.1 %collective-permute-start.1 = (bf16[8,64,128]{2,1,0:T(8,128)(2,1)S(1)}, bf16[8,64,128]{2,1,0:T(8,128)(2,1)S(1)}, u32[]{:S(2)}, u32[]{:S(2)}) collective-permute-start(bf16[8,64,128]{2,1,0:T(8,128)(2,1)S(1)} %get-tuple-element.31), channel_id=1, source_target_pairs={{0,2},{2,0},{4,6},{6,4},{8,10},{10,8},{12,14},{14,12},{16,18},{18,... | collective-permute-start | bytes 393224 | tf_op jit(solution)/shard_map/ppermute | solution.py:220
  6.3 17.2 %copy-start = (bf16[1024,128]{1,0:T(8,128)(2,1)S(1)}, bf16[1024,128]{1,0:T(8,128)(2,1)}, u32[]{:S(2)}) copy-start(bf16[1024,128]{1,0:T(8,128)(2,1)} %og_ref.1) | copy-start | bytes 786436
  6.3 17.2 %copy-start.1 = (bf16[128,128]{1,0:T(8,128)(2,1)S(1)}, bf16[128,128]{1,0:T(8,128)(2,1)}, u32[]{:S(2)}) copy-start(bf16[128,128]{1,0:T(8,128)(2,1)} %w_ref.1) | copy-start | bytes 98308
  6.4 17.2 %copy-start.2 = (f32[128]{0:T(128)S(1)}, f32[128]{0:T(128)}, u32[]{:S(2)}) copy-start(f32[128]{0:T(128)} %param.10) | copy-start | bytes 1540
  6.4 7.2 %collective-permute-start = (bf16[8,64,128]{2,1,0:T(8,128)(2,1)S(1)}, bf16[8,64,128]{2,1,0:T(8,128)(2,1)S(1)}, u32[]{:S(2)}, u32[]{:S(2)}) collective-permute-start(bf16[8,64,128]{2,1,0:T(8,128)(2,1)S(1)} %get-tuple-element.29), channel_id=1, source_target_pairs={{0,2},{2,8},{4,6},{6,12},{8,10},{10,16},{12,14},{14,20},{16,18},{1... | collective-permute-start | bytes 393224 | tf_op jit(solution)/shard_map/ppermute | solution.py:220
  6.5 11.4 %collective-permute-start.2 = (bf16[8,64,128]{2,1,0:T(8,128)(2,1)S(1)}, bf16[8,64,128]{2,1,0:T(8,128)(2,1)S(1)}, u32[]{:S(2)}, u32[]{:S(2)}) collective-permute-start(bf16[8,64,128]{2,1,0:T(8,128)(2,1)S(1)} %shard_map.114), channel_id=1, source_target_pairs={{0,4},{2,6},{4,8},{6,10},{8,12},{10,14},{12,16},{14,18},{16,20},{1... | collective-permute-start | bytes 393224 | tf_op jit(solution)/shard_map/ppermute | solution.py:220
  17.9 5.6 %collective-permute-start.3 = (bf16[8,64,128]{2,1,0:T(8,128)(2,1)S(1)}, bf16[8,64,128]{2,1,0:T(8,128)(2,1)S(1)}, u32[]{:S(2)}, u32[]{:S(2)}) collective-permute-start(bf16[8,64,128]{2,1,0:T(8,128)(2,1)S(1)} %shard_map.115.refs_0_), channel_id=1, source_target_pairs={{0,1},{1,0},{2,3},{3,2},{4,5},{5,4},{6,7},{7,6},{8,9},{9,8},{10,11... | collective-permute-start | bytes 393224 | tf_op jit(solution)/shard_map/ppermute | solution.py:220
  25.2 5.0 %collective-permute-start.4 = (bf16[8,64,128]{2,1,0:T(8,128)(2,1)S(1)}, bf16[8,64,128]{2,1,0:T(8,128)(2,1)S(1)}, u32[]{:S(2)}, u32[]{:S(2)}) collective-permute-start(bf16[8,64,128]{2,1,0:T(8,128)(2,1)S(1)} %get-tuple-element.39), channel_id=1, source_target_pairs={{0,1},{1,0},{2,3},{3,2},{4,5},{5,4},{6,7},{7,6},{8,9},{9,8},{10,11... | collective-permute-start | bytes 393224 | tf_op jit(solution)/shard_map/ppermute | solution.py:220
  30.2 6.2 %collective-permute-start.5 = (bf16[8,64,128]{2,1,0:T(8,128)(2,1)S(1)}, bf16[8,64,128]{2,1,0:T(8,128)(2,1)S(1)}, u32[]{:S(2)}, u32[]{:S(2)}) collective-permute-start(bf16[8,64,128]{2,1,0:T(8,128)(2,1)S(1)} %shard_map.118.g0), channel_id=1, source_target_pairs={{0,28},{2,30},{4,0},{6,2},{8,4},{10,6},{12,8},{14,10},{16,12},{18,... | collective-permute-start | bytes 393224 | tf_op jit(solution)/shard_map/ppermute | solution.py:220
  30.5 12.0 %collective-permute-start.7 = (bf16[8,64,128]{2,1,0:T(8,128)(2,1)S(1)}, bf16[8,64,128]{2,1,0:T(8,128)(2,1)S(1)}, u32[]{:S(2)}, u32[]{:S(2)}) collective-permute-start(bf16[8,64,128]{2,1,0:T(8,128)(2,1)S(1)} %shard_map.118.g0), channel_id=1, source_target_pairs={{0,26},{2,0},{4,30},{6,4},{8,2},{10,8},{12,6},{14,12},{16,10},{18,... | collective-permute-start | bytes 393224 | tf_op jit(solution)/shard_map/ppermute | solution.py:220
  31.1 5.3 %collective-permute-start.8 = (f32[136,128]{1,0:T(8,128)S(1)}, f32[136,128]{1,0:T(8,128)S(1)}, u32[]{:S(2)}, u32[]{:S(2)}) collective-permute-start(f32[136,128]{1,0:T(8,128)S(1)} %get-tuple-element.42.refs_0_), channel_id=1, source_target_pairs={{0,2},{2,4},{4,6},{6,0},{8,10},{10,12},{12,14},{14,8},{16,18},{18,... | collective-permute-start | bytes 208904 | tf_op jit(solution)/shard_map/ppermute | solution.py:220
  31.1 6.4 %collective-permute-start.9 = (f32[136,128]{1,0:T(8,128)S(1)}, f32[136,128]{1,0:T(8,128)S(1)}, u32[]{:S(2)}, u32[]{:S(2)}) collective-permute-start(f32[136,128]{1,0:T(8,128)S(1)} %get-tuple-element.42.refs_0_), channel_id=1, source_target_pairs={{0,4},{2,6},{4,0},{6,2},{8,12},{10,14},{12,8},{14,10},{16,20},{18,... | collective-permute-start | bytes 208904 | tf_op jit(solution)/shard_map/ppermute | solution.py:220
  32.8 4.7 %collective-permute-start.10 = (f32[136,128]{1,0:T(8,128)S(1)}, f32[136,128]{1,0:T(8,128)S(1)}, u32[]{:S(2)}, u32[]{:S(2)}) collective-permute-start(f32[136,128]{1,0:T(8,128)S(1)} %get-tuple-element.42.refs_0_), channel_id=1, source_target_pairs={{0,6},{2,0},{4,2},{6,4},{8,14},{10,8},{12,10},{14,12},{16,22},{18,... | collective-permute-start | bytes 208904 | tf_op jit(solution)/shard_map/ppermute | solution.py:220
  36.4 10.1 %collective-permute-start.6 = (bf16[8,64,128]{2,1,0:T(8,128)(2,1)S(1)}, bf16[8,64,128]{2,1,0:T(8,128)(2,1)S(1)}, u32[]{:S(2)}, u32[]{:S(2)}) collective-permute-start(bf16[8,64,128]{2,1,0:T(8,128)(2,1)S(1)} %collective-permute-done.5.g2), channel_id=1, source_target_pairs={{0,2},{2,0},{4,6},{6,4},{8,10},{10,8},{12,14},{14,12},{16,18},{18,... | collective-permute-start | bytes 393224 | tf_op jit(solution)/shard_map/ppermute | solution.py:220
  37.5 6.9 %collective-permute-start.11 = (f32[136,128]{1,0:T(8,128)S(1)}, f32[136,128]{1,0:T(8,128)S(1)}, u32[]{:S(2)}, u32[]{:S(2)}) collective-permute-start(f32[136,128]{1,0:T(8,128)S(1)} %shard_map.121.refs_0_), channel_id=1, source_target_pairs={{0,8},{2,10},{4,12},{6,14},{8,16},{10,18},{12,20},{14,22},{16,24},... | collective-permute-start | bytes 208904 | tf_op jit(solution)/shard_map/ppermute | solution.py:220
  37.6 8.9 %collective-permute-start.12 = (f32[136,128]{1,0:T(8,128)S(1)}, f32[136,128]{1,0:T(8,128)S(1)}, u32[]{:S(2)}, u32[]{:S(2)}) collective-permute-start(f32[136,128]{1,0:T(8,128)S(1)} %shard_map.121.refs_0_), channel_id=1, source_target_pairs={{0,16},{2,18},{4,20},{6,22},{8,24},{10,26},{12,28},{14,30},{16,0},... | collective-permute-start | bytes 208904 | tf_op jit(solution)/shard_map/ppermute | solution.py:220
  39.7 6.8 %collective-permute-start.13 = (f32[136,128]{1,0:T(8,128)S(1)}, f32[136,128]{1,0:T(8,128)S(1)}, u32[]{:S(2)}, u32[]{:S(2)}) collective-permute-start(f32[136,128]{1,0:T(8,128)S(1)} %shard_map.121.refs_0_), channel_id=1, source_target_pairs={{0,24},{2,26},{4,28},{6,30},{8,0},{10,2},{12,4},{14,6},{16,8},{18,... | collective-permute-start | bytes 208904 | tf_op jit(solution)/shard_map/ppermute | solution.py:220

commit v2 on v1

--- a/solution.py
+++ b/solution.py
@@ -211,6 +211,12 @@
     return functools.reduce(lambda a, b: a + b, parts)
 
 
+def piece_sum_kernel(pieces, out):
+    total = functools.reduce(lambda a, b: a + b, [pieces[i] for i in range(pieces.shape[0])])
+    for i in range(pieces.shape[0]):
+        out[i] = total
+
+
 def paired_sum_kernel(*refs):
     refs[-1][...] = paired_sum([r[...] for r in refs[:-1]])
 
@@ -252,7 +258,7 @@
     tiles = jax.ShapeDtypeStruct((groups, REACH, BLOCK, BLOCK), BF16)
     slots = jax.ShapeDtypeStruct((capacity,), jnp.int32)
     rows = jax.ShapeDtypeStruct((nodes, hid), BF16)
-    gradient = jax.ShapeDtypeStruct((f_in + 8, hid), F32)
+    gradient = jax.ShapeDtypeStruct((f_in + 128, hid), F32)
     m = groups_at_once(groups)
     flops = 2 * capacity * BLOCK * BLOCK * width // REACH
 
@@ -285,7 +291,7 @@
     hs = [h] + [moved(h, "feat", lambda i, q=q: i - q) for q in range(1, parts)]
     act, ht, grads, g_own, *g_others = call(
         functools.partial(middle_kernel, parts),
-        [rows, jax.ShapeDtypeStruct((f_in + 16, nodes), BF16), rows, wide] + [piece] * (parts - 1),
+        [rows, jax.ShapeDtypeStruct((f_in + 128, nodes), BF16), rows, wide] + [piece] * (parts - 1),
         [VMEM] * (3 + parts),
         [VMEM] * (3 + parts),
         (),
@@ -304,12 +310,11 @@
     (g,) = call(functools.partial(sum_kernel, parts), [piece], [VMEM] * parts, [VMEM])(g_own, *g_received)
     g_chip = moved(g, "dom", lambda i: i - 2)
     g_direct = moved(g, "dom", lambda i: i - 3 + 2 * (i % 2))
-    wgs, stride = [wg], 1
-    for r in radices(lax.axis_size("dom")):
-        if len(wgs) > 1:
-            (wg,) = call(paired_sum_kernel, [gradient], [VMEM] * len(wgs), [VMEM])(*wgs)
-        wgs = exchanged(wg, "dom", stride, r)
-        stride *= r
+    n = lax.axis_size("dom")
+    pieces = lax.all_to_all(wg.reshape(n, -1, hid), "dom", 0, 0)
+    (wg,) = call(piece_sum_kernel, [jax.ShapeDtypeStruct(pieces.shape, F32)], [VMEM], [VMEM])(pieces)
+    wg = lax.all_to_all(wg, "dom", 0, 0).reshape(gradient.shape)
+    wgs = [wg]
     (back0,) = call(backward_own_kernel, [totals], [SMEM] * 3 + [VMEM] * 2, [VMEM], (), flops)(*index, tiles, g)
     g_swap = moved(g_chip, "dom", swapped)
     back2, backd = call(

time: 48.5 us -> 62.2 us (1.28); the launches traced: 48.4 us -> 61.3 us
  starting transfers between devices: 14.4 us -> 21.2 us
  Pallas kernels: 12.5 us -> 18.5 us
  local copies, waits for them, and re-layouts: 0.02 us -> 5.6 us
  waiting for transfers between devices: 20.1 us -> 14.6 us
    all_to_all x0 -> x2, starting transfers between devices: none -> 7.68 us  [the longest x1 4.17 us: shards(): wg = lax.all_to_all(wg, 'dom', 0, 0).reshape(gradient.shape)]
    unnamed x6 -> x22, local copies, waits for them, and re-layouts: 0.02 us -> 5.6 us
    ppermute x14 -> x8, waiting for transfers between devices: 20.1 us -> 14.6 us  [moved(): return lax.ppermute(block, axis, [(i, target(i) % n) for i in range(n)])]
    pallas_call x1, Pallas kernels: 1.23 us -> 2.19 us  [shards(): call(backward_near_kernel, [totals, totals], [SMEM] * 3 + [VMEM] * 3, [VM...]
    pallas_call x1, Pallas kernels: 1.11 us -> 2 us  [shards(): call(backward_own_kernel, [totals], [SMEM] * 3 + [VMEM] * 2, [VMEM], (),...]
    ppermute x14 -> x8, starting transfers between devices: 14.4 us -> 13.5 us  [moved(): return lax.ppermute(block, axis, [(i, target(i) % n) for i in range(n)])]
    pallas_call x1, Pallas kernels: 1.88 us -> 2.73 us  [shards(): call(backward_last_kernel, [jax.ShapeDtypeStruct((width, nodes), BF16), j...]
    pallas_call x1, Pallas kernels: 1.47 us -> 2.3 us  [shards(): call(forward_send_kernel, [totals, piece], [SMEM] * 3 + [VMEM] * 2, [VMEM...]
  transfers between devices with their start and end apart: 14 -> 10, of which waited for: 8 -> 5; matrix products, arithmetic and copies ran while one was open for 0% -> 0% of each run, Pallas kernels for 12% -> 16%
where the time goes in v2:
time: 62.2 us; the launch traced here: 61.3 us
  starting transfers between devices  21.2 us (34%)
  Pallas kernels  18.5 us (30%)
  waiting for transfers between devices  14.6 us (23%)
  local copies, waits for them, and re-layouts  5.6 us (9%)
  between operations  1.45 us (2%)
    ppermute x8, waiting for transfers between devices, moved(): return lax.ppermute(block, axis, [(i, target(i) % n) for i in range(n)])  14.6 us
    ppermute x8, starting transfers between devices, moved(): return lax.ppermute(block, axis, [(i, target(i) % n) for i in range(n)])  13.5 us
    unnamed x22, local copies, waits for them, and re-layouts  5.6 us
    all_to_all x1, starting transfers between devices, shards(): wg = lax.all_to_all(wg, 'dom', 0, 0).reshape(gradient.shape)  4.17 us
    pallas_call x1, Pallas kernels, shards(): call(forward_swap_kernel, [tiles, piece, piece, slots, slots], [SMEM] + [...  3.64 us
    all_to_all x1, starting transfers between devices, shards(): pieces = lax.all_to_all(wg.reshape(n, -1, hid), 'dom', 0, 0)  3.51 us
    pallas_call x1, Pallas kernels, shards(): call(backward_last_kernel, [jax.ShapeDtypeStruct((width, nodes), BF16), j...  2.73 us
    pallas_call x1, Pallas kernels, shards(): call(forward_send_kernel, [totals, piece], [SMEM] * 3 + [VMEM] * 2, [VMEM...  2.3 us
  transfers between devices with their start and end apart: 10, of which 5 were waited for; matrix products, arithmetic and copies ran while one was open for 0% of the time, Pallas kernels for 16%

profile of v2, /device:TPU:0, one launch (start us, length us, event | category | flops | bytes accessed | tf_op | source)
XLA Modules:
  0.0 61.3 jit_solution(9968518395482014370)
XLA Ops:
  1.3 3.6 %shard_map.111 = (bf16[24,4,128,128]{3,2,1,0:T(8,128)(2,1)S(1)}, bf16[8,64,128]{2,1,0:T(8,128)(2,1)S(1)}, bf16[8,64,128]{2,1,0:T(8,128)(2,1)S(1)}, s32[96]{0:T(128)S(1)}, s32[96]{0:T(128)S(1)}) custom-call(s32[1]{0:T(128)S(6)} %copy.12.count, s32[96]{0:T(128)} %src_hbm.1, s32[96]{0:T(128)} %dst_hbm.1, bf16[1024,128]{1,0:T(8,128)(2,1)} %x_hbm.1, ...), custom_call_target="tpu_custom_call" | custom-call | flops 50331648 | bytes 1048576 | tf_op jit(solution)/shard_map/pallas_call | solution.py:268
  5.0 2.3 %shard_map.113 = (f32[9,64,128]{2,1,0:T(8,128)S(1)}, bf16[8,64,128]{2,1,0:T(8,128)(2,1)S(1)}) custom-call(s32[1]{0:T(128)S(6)} %copy.12.count, s32[96]{0:T(128)S(1)} %get-tuple-element.25.src, s32[96]{0:T(128)S(1)} %get-tuple-element.26.dst, bf16[8,64,128]{2,1,0:T(8,128)(2,1)S(1)} %get-tuple-element.27.xt, bf16[24,4,128,128]{3,2,1,0:T(8,128)(2,1)S(1)} %get-tuple-element.28.tiles), custom_call_target="tpu_custom_call" | custom-call | flops 100663296 | bytes 1048576 | tf_op jit(solution)/shard_map/pallas_call | solution.py:283
  7.5 1.8 %collective-permute-start.2 = (bf16[8,64,128]{2,1,0:T(8,128)(2,1)S(1)}, bf16[8,64,128]{2,1,0:T(8,128)(2,1)S(1)}, u32[]{:S(2)}, u32[]{:S(2)}) collective-permute-start(bf16[8,64,128]{2,1,0:T(8,128)(2,1)S(1)} %shard_map.114), channel_id=1, source_target_pairs={{0,4},{2,6},{4,8},{6,10},{8,12},{10,14},{12,16},{14,18},{16,20},{1... | collective-permute-start | bytes 393224 | tf_op jit(solution)/shard_map/ppermute | solution.py:226
  9.3 1.8 %shard_map.112.refs_0_ = f32[9,64,128]{2,1,0:T(8,128)S(1)} custom-call(s32[1]{0:T(128)S(6)} %copy.12.count, s32[96]{0:T(128)S(1)} %get-tuple-element.25.src, s32[96]{0:T(128)S(1)} %get-tuple-element.26.dst, bf16[8,64,128]{2,1,0:T(8,128)(2,1)S(1)} %get-tuple-element.27.xt, bf16[24,4,128,128]{3,2,1,0:T(8,128)(2,1)S(1)} %get-tuple-element.28.tiles), custom_call_target="tpu_custom_call" | custom-call | flops 50331648 | bytes 1048576 | tf_op jit(solution)/shard_map/pallas_call | solution.py:289
  11.1 2.5 %collective-permute-done.refs_1_ = bf16[8,64,128]{2,1,0:T(8,128)(2,1)S(1)} collective-permute-done((bf16[8,64,128]{2,1,0:T(8,128)(2,1)S(1)}, bf16[8,64,128]{2,1,0:T(8,128)(2,1)S(1)}, u32[]{:S(2)}, u32[]{:S(2)}) %collective-permute-start) | collective-permute-done | bytes 131104 | tf_op jit(solution)/shard_map/ppermute | solution.py:226
  13.6 2.9 %collective-permute-done.2.refs_2_ = bf16[8,64,128]{2,1,0:T(8,128)(2,1)S(1)} collective-permute-done((bf16[8,64,128]{2,1,0:T(8,128)(2,1)S(1)}, bf16[8,64,128]{2,1,0:T(8,128)(2,1)S(1)}, u32[]{:S(2)}, u32[]{:S(2)}) %collective-permute-start.2) | collective-permute-done | bytes 131104 | tf_op jit(solution)/shard_map/ppermute | solution.py:226
  16.6 2.4 %collective-permute-start.3 = (bf16[8,64,128]{2,1,0:T(8,128)(2,1)S(1)}, bf16[8,64,128]{2,1,0:T(8,128)(2,1)S(1)}, u32[]{:S(2)}, u32[]{:S(2)}) collective-permute-start(bf16[8,64,128]{2,1,0:T(8,128)(2,1)S(1)} %shard_map.115.refs_0_), channel_id=1, source_target_pairs={{0,1},{1,0},{2,3},{3,2},{4,5},{5,4},{6,7},{7,6},{8,9},{9,8},{10,11... | collective-permute-start | bytes 393224 | tf_op jit(solution)/shard_map/ppermute | solution.py:226
  19.0 3.7 %collective-permute-done.3.refs_1_ = bf16[8,64,128]{2,1,0:T(8,128)(2,1)S(1)} collective-permute-done((bf16[8,64,128]{2,1,0:T(8,128)(2,1)S(1)}, bf16[8,64,128]{2,1,0:T(8,128)(2,1)S(1)}, u32[]{:S(2)}, u32[]{:S(2)}) %collective-permute-start.3) | collective-permute-done | bytes 131104 | tf_op jit(solution)/shard_map/ppermute | solution.py:226
  22.7 1.7 %shard_map.116 = (bf16[1024,128]{1,0:T(8,128)(2,1)S(1)}, bf16[256,1024]{1,0:T(8,128)(2,1)S(1)}, bf16[1024,128]{1,0:T(8,128)(2,1)S(1)}, f32[8,64,128]{2,1,0:T(8,128)S(1)}, bf16[8,64,128]{2,1,0:T(8,128)(2,1)S(1)}) custom-call(f32[1,128]{1,0:T(1,128)S(1)} %bitcast.7, bf16[128,128]{1,0:T(8,128)(2,1)S(1)} %copy-done.8, bf16[1024,128]{1,0:T(8,128)(2,1)S(1)} %copy-done.4, ...), custom_call_target="tpu_custom_call" | custom-call | flops 67108864 | bytes 1048576 | tf_op jit(solution)/shard_map/pallas_call | solution.py:292
  24.4 0.7 %shard_map.117 = (bf16[1024,128]{1,0:T(8,128)(2,1)}, f32[256,128]{1,0:T(8,128)S(1)}) custom-call(bf16[256,1024]{1,0:T(8,128)(2,1)S(1)} %get-tuple-element.32.ht, bf16[1024,128]{1,0:T(8,128)(2,1)S(1)} %get-tuple-element.33.grads, bf16[1024,128]{1,0:T(8,128)(2,1)S(1)} %get-tuple-element.34.act), custom_call_target="tpu_custom_call" | custom-call | flops 33554432 | bytes 1048576 | tf_op jit(solution)/shard_map/pallas_call | solution.py:301
  25.8 3.5 %all-to-all-start = ((f32[16,16,128]{2,1,0:T(8,128)}), f32[16,16,128]{2,1,0:T(8,128)S(1)}, u32[]{:S(2)}, u32[]{:S(2)}) async-start(f32[16,16,128]{2,1,0:T(8,128)} %bitcast.6), calls=%async_computation | async-start | bytes 262144 | tf_op jit(solution)/shard_map/all_to_all | solution.py:314
  29.4 1.3 %collective-permute-start.4 = (bf16[8,64,128]{2,1,0:T(8,128)(2,1)}, bf16[8,64,128]{2,1,0:T(8,128)(2,1)S(1)}, u32[]{:S(2)}, u32[]{:S(2)}) collective-permute-start(bf16[8,64,128]{2,1,0:T(8,128)(2,1)} %copy-done.10), channel_id=1, source_target_pairs={{0,1},{1,0},{2,3},{3,2},{4,5},{5,4},{6,7},{7,6},{8,9},{9,8},{10,11... | collective-permute-start | bytes 393224 | tf_op jit(solution)/shard_map/ppermute | solution.py:226
  30.7 4.6 %collective-permute-done.4.refs_1_ = bf16[8,64,128]{2,1,0:T(8,128)(2,1)S(1)} collective-permute-done((bf16[8,64,128]{2,1,0:T(8,128)(2,1)}, bf16[8,64,128]{2,1,0:T(8,128)(2,1)S(1)}, u32[]{:S(2)}, u32[]{:S(2)}) %collective-permute-start.4) | collective-permute-done | bytes 131104 | tf_op jit(solution)/shard_map/ppermute | solution.py:226
  36.0 4.5 %collective-permute-start.5 = (bf16[8,64,128]{2,1,0:T(8,128)(2,1)}, bf16[8,64,128]{2,1,0:T(8,128)(2,1)}, u32[]{:S(2)}, u32[]{:S(2)}) collective-permute-start(bf16[8,64,128]{2,1,0:T(8,128)(2,1)} %shard_map.118.g0), channel_id=1, source_target_pairs={{0,28},{2,30},{4,0},{6,2},{8,4},{10,6},{12,8},{14,10},{16,12},{18,... | collective-permute-start | bytes 393224 | tf_op jit(solution)/shard_map/ppermute | solution.py:226
  41.1 4.2 %all-to-all-start.1 = ((f32[16,16,128]{2,1,0:T(8,128)}), f32[16,16,128]{2,1,0:T(8,128)}, u32[]{:S(2)}, u32[]{:S(2)}) async-start(f32[16,16,128]{2,1,0:T(8,128)} %shard_map.121), calls=%async_computation.1 | async-start | bytes 262144 | tf_op jit(solution)/shard_map/all_to_all | solution.py:316
  45.3 3.4 %collective-permute-start.7 = (bf16[8,64,128]{2,1,0:T(8,128)(2,1)}, bf16[8,64,128]{2,1,0:T(8,128)(2,1)S(1)}, u32[]{:S(2)}, u32[]{:S(2)}) collective-permute-start(bf16[8,64,128]{2,1,0:T(8,128)(2,1)} %shard_map.118.g0), channel_id=1, source_target_pairs={{0,26},{2,0},{4,30},{6,4},{8,2},{10,8},{12,6},{14,12},{16,10},{18,... | collective-permute-start | bytes 393224 | tf_op jit(solution)/shard_map/ppermute | solution.py:226
  48.6 2.0 %shard_map.119.acc0 = f32[9,64,128]{2,1,0:T(8,128)S(1)} custom-call(s32[1]{0:T(128)S(6)} %copy.12.count, s32[96]{0:T(128)S(1)} %get-tuple-element.25.src, s32[96]{0:T(128)S(1)} %get-tuple-element.26.dst, bf16[24,4,128,128]{3,2,1,0:T(8,128)(2,1)S(1)} %get-tuple-element.28.tiles, bf16[8,64,128]{2,1,0:T(8,128)(2,1)} %shard_map.118.g0), custom_call_target="tpu_custom_call" | custom-call | flops 50331648 | bytes 1048576 | tf_op jit(solution)/shard_map/pallas_call | solution.py:318
  50.6 0.8 %collective-permute-done.7.gd = bf16[8,64,128]{2,1,0:T(8,128)(2,1)S(1)} collective-permute-done((bf16[8,64,128]{2,1,0:T(8,128)(2,1)}, bf16[8,64,128]{2,1,0:T(8,128)(2,1)S(1)}, u32[]{:S(2)}, u32[]{:S(2)}) %collective-permute-start.7) | collective-permute-done | bytes 131104 | tf_op jit(solution)/shard_map/ppermute | solution.py:226
  51.5 2.2 %shard_map.120 = (f32[9,64,128]{2,1,0:T(8,128)S(1)}, f32[9,64,128]{2,1,0:T(8,128)S(1)}) custom-call(s32[1]{0:T(128)S(6)} %copy.12.count, s32[96]{0:T(128)S(1)} %get-tuple-element.25.src, s32[96]{0:T(128)S(1)} %get-tuple-element.26.dst, bf16[24,4,128,128]{3,2,1,0:T(8,128)(2,1)S(1)} %get-tuple-element.28.tiles, bf16[8,64,128]{2,1,0:T(8,128)(2,1)} %collective-permute-done.5.g2, ...), custom_call_target="tpu_custom_call" | custom-call | flops 100663296 | bytes 1048576 | tf_op jit(solution)/shard_map/pallas_call | solution.py:320
  54.4 0.7 %copy-done.2 = f32[9,64,128]{2,1,0:T(8,128)} copy-done((f32[9,64,128]{2,1,0:T(8,128)}, f32[9,64,128]{2,1,0:T(8,128)S(1)}, u32[]{:S(2)}) %copy-start.2) | copy-done | bytes 294936
  55.8 1.0 %copy-done.1 = f32[9,64,128]{2,1,0:T(8,128)S(1)} copy-done((f32[9,64,128]{2,1,0:T(8,128)S(1)}, f32[9,64,128]{2,1,0:T(8,128)}, u32[]{:S(2)}) %copy-start.1) | copy-done | bytes 294936
  56.7 1.0 %copy-done.3 = f32[9,64,128]{2,1,0:T(8,128)S(1)} copy-done((f32[9,64,128]{2,1,0:T(8,128)S(1)}, f32[9,64,128]{2,1,0:T(8,128)}, u32[]{:S(2)}) %copy-start.3) | copy-done | bytes 294936
  57.7 0.9 %copy-done.6 = bf16[8,64,128]{2,1,0:T(8,128)(2,1)S(1)} copy-done((bf16[8,64,128]{2,1,0:T(8,128)(2,1)S(1)}, bf16[8,64,128]{2,1,0:T(8,128)(2,1)}, u32[]{:S(2)}) %copy-start.6) | copy-done | bytes 131096
  58.6 2.7 %shard_map.122 = (bf16[64,1024]{1,0:T(8,128)(2,1)}, f32[128,128]{1,0:T(8,128)}, f32[1,128]{1,0:T(1,128)}) custom-call(s32[1]{0:T(128)S(6)} %copy.12.count, s32[96]{0:T(128)S(1)} %get-tuple-element.25.src, s32[96]{0:T(128)S(1)} %get-tuple-element.26.dst, bf16[24,4,128,128]{3,2,1,0:T(8,128)(2,1)S(1)} %get-tuple-element.28.tiles, ...), custom_call_target="tpu_custom_call" | custom-call | flops 50331648 | bytes 1048576 | tf_op jit(solution)/shard_map/pallas_call | solution.py:323
  (30 shorter events, 3.6 us)
Async XLA Ops:
  4.9 2.5 %collective-permute-start.1 = (bf16[8,64,128]{2,1,0:T(8,128)(2,1)S(1)}, bf16[8,64,128]{2,1,0:T(8,128)(2,1)S(1)}, u32[]{:S(2)}, u32[]{:S(2)}) collective-permute-start(bf16[8,64,128]{2,1,0:T(8,128)(2,1)S(1)} %get-tuple-element.31), channel_id=1, source_target_pairs={{0,2},{2,0},{4,6},{6,4},{8,10},{10,8},{12,14},{14,12},{16,18},{18,... | collective-permute-start | bytes 393224 | tf_op jit(solution)/shard_map/ppermute | solution.py:226
  7.3 15.4 %copy-start.4 = (bf16[1024,128]{1,0:T(8,128)(2,1)S(1)}, bf16[1024,128]{1,0:T(8,128)(2,1)}, u32[]{:S(2)}) copy-start(bf16[1024,128]{1,0:T(8,128)(2,1)} %og_ref.1) | copy-start | bytes 786436
  7.3 15.4 %copy-start.8 = (bf16[128,128]{1,0:T(8,128)(2,1)S(1)}, bf16[128,128]{1,0:T(8,128)(2,1)}, u32[]{:S(2)}) copy-start(bf16[128,128]{1,0:T(8,128)(2,1)} %w_ref.1) | copy-start | bytes 98308
  7.3 15.4 %copy-start.9 = (f32[128]{0:T(128)S(1)}, f32[128]{0:T(128)}, u32[]{:S(2)}) copy-start(f32[128]{0:T(128)} %param.10) | copy-start | bytes 1540
  7.4 6.2 %collective-permute-start = (bf16[8,64,128]{2,1,0:T(8,128)(2,1)S(1)}, bf16[8,64,128]{2,1,0:T(8,128)(2,1)S(1)}, u32[]{:S(2)}, u32[]{:S(2)}) collective-permute-start(bf16[8,64,128]{2,1,0:T(8,128)(2,1)S(1)} %get-tuple-element.29), channel_id=1, source_target_pairs={{0,2},{2,8},{4,6},{6,12},{8,10},{10,16},{12,14},{14,20},{16,18},{1... | collective-permute-start | bytes 393224 | tf_op jit(solution)/shard_map/ppermute | solution.py:226
  7.5 9.1 %collective-permute-start.2 = (bf16[8,64,128]{2,1,0:T(8,128)(2,1)S(1)}, bf16[8,64,128]{2,1,0:T(8,128)(2,1)S(1)}, u32[]{:S(2)}, u32[]{:S(2)}) collective-permute-start(bf16[8,64,128]{2,1,0:T(8,128)(2,1)S(1)} %shard_map.114), channel_id=1, source_target_pairs={{0,4},{2,6},{4,8},{6,10},{8,12},{10,14},{12,16},{14,18},{16,20},{1... | collective-permute-start | bytes 393224 | tf_op jit(solution)/shard_map/ppermute | solution.py:226
  16.6 6.2 %collective-permute-start.3 = (bf16[8,64,128]{2,1,0:T(8,128)(2,1)S(1)}, bf16[8,64,128]{2,1,0:T(8,128)(2,1)S(1)}, u32[]{:S(2)}, u32[]{:S(2)}) collective-permute-start(bf16[8,64,128]{2,1,0:T(8,128)(2,1)S(1)} %shard_map.115.refs_0_), channel_id=1, source_target_pairs={{0,1},{1,0},{2,3},{3,2},{4,5},{5,4},{6,7},{7,6},{8,9},{9,8},{10,11... | collective-permute-start | bytes 393224 | tf_op jit(solution)/shard_map/ppermute | solution.py:226
  24.4 0.8 %copy-start.10 = (bf16[8,64,128]{2,1,0:T(8,128)(2,1)}, bf16[8,64,128]{2,1,0:T(8,128)(2,1)S(1)}, u32[]{:S(2)}) copy-start(bf16[8,64,128]{2,1,0:T(8,128)(2,1)S(1)} %get-tuple-element.39) | copy-start | bytes 393220
  25.2 0.7 %copy-start.7 = (f32[256,128]{1,0:T(8,128)}, f32[256,128]{1,0:T(8,128)S(1)}, u32[]{:S(2)}) copy-start(f32[256,128]{1,0:T(8,128)S(1)} %get-tuple-element.42) | copy-start | bytes 393220
  25.8 14.6 %all-to-all-start = ((f32[16,16,128]{2,1,0:T(8,128)}), f32[16,16,128]{2,1,0:T(8,128)S(1)}, u32[]{:S(2)}, u32[]{:S(2)}) async-start(f32[16,16,128]{2,1,0:T(8,128)} %bitcast.6), calls=%async_computation | async-start | bytes 262144 | tf_op jit(solution)/shard_map/all_to_all | solution.py:314
  29.4 5.9 %collective-permute-start.4 = (bf16[8,64,128]{2,1,0:T(8,128)(2,1)}, bf16[8,64,128]{2,1,0:T(8,128)(2,1)S(1)}, u32[]{:S(2)}, u32[]{:S(2)}) collective-permute-start(bf16[8,64,128]{2,1,0:T(8,128)(2,1)} %copy-done.10), channel_id=1, source_target_pairs={{0,1},{1,0},{2,3},{3,2},{4,5},{5,4},{6,7},{7,6},{8,9},{9,8},{10,11... | collective-permute-start | bytes 393224 | tf_op jit(solution)/shard_map/ppermute | solution.py:226
  36.0 12.7 %collective-permute-start.5 = (bf16[8,64,128]{2,1,0:T(8,128)(2,1)}, bf16[8,64,128]{2,1,0:T(8,128)(2,1)}, u32[]{:S(2)}, u32[]{:S(2)}) collective-permute-start(bf16[8,64,128]{2,1,0:T(8,128)(2,1)} %shard_map.118.g0), channel_id=1, source_target_pairs={{0,28},{2,30},{4,0},{6,2},{8,4},{10,6},{12,8},{14,10},{16,12},{18,... | collective-permute-start | bytes 393224 | tf_op jit(solution)/shard_map/ppermute | solution.py:226
  41.1 14.7 %all-to-all-start.1 = ((f32[16,16,128]{2,1,0:T(8,128)}), f32[16,16,128]{2,1,0:T(8,128)}, u32[]{:S(2)}, u32[]{:S(2)}) async-start(f32[16,16,128]{2,1,0:T(8,128)} %shard_map.121), calls=%async_computation.1 | async-start | bytes 262144 | tf_op jit(solution)/shard_map/all_to_all | solution.py:316
  45.3 6.2 %collective-permute-start.7 = (bf16[8,64,128]{2,1,0:T(8,128)(2,1)}, bf16[8,64,128]{2,1,0:T(8,128)(2,1)S(1)}, u32[]{:S(2)}, u32[]{:S(2)}) collective-permute-start(bf16[8,64,128]{2,1,0:T(8,128)(2,1)} %shard_map.118.g0), channel_id=1, source_target_pairs={{0,26},{2,0},{4,30},{6,4},{8,2},{10,8},{12,6},{14,12},{16,10},{18,... | collective-permute-start | bytes 393224 | tf_op jit(solution)/shard_map/ppermute | solution.py:226
  48.6 6.5 %collective-permute-start.6 = (bf16[8,64,128]{2,1,0:T(8,128)(2,1)}, bf16[8,64,128]{2,1,0:T(8,128)(2,1)S(1)}, u32[]{:S(2)}, u32[]{:S(2)}) collective-permute-start(bf16[8,64,128]{2,1,0:T(8,128)(2,1)} %collective-permute-done.5.g2), channel_id=1, source_target_pairs={{0,2},{2,0},{4,6},{6,4},{8,10},{10,8},{12,14},{14,12},{16,18},{18,... | collective-permute-start | bytes 393224 | tf_op jit(solution)/shard_map/ppermute | solution.py:226
  53.7 0.7 %copy-start = (f32[9,64,128]{2,1,0:T(8,128)}, f32[9,64,128]{2,1,0:T(8,128)S(1)}, u32[]{:S(2)}) copy-start(f32[9,64,128]{2,1,0:T(8,128)S(1)} %get-tuple-element.40.acc2) | copy-start | bytes 884740
  54.4 0.7 %copy-start.2 = (f32[9,64,128]{2,1,0:T(8,128)}, f32[9,64,128]{2,1,0:T(8,128)S(1)}, u32[]{:S(2)}) copy-start(f32[9,64,128]{2,1,0:T(8,128)S(1)} %get-tuple-element.41.accd) | copy-start | bytes 884740
  55.1 0.7 %copy-start.5 = (bf16[8,64,128]{2,1,0:T(8,128)(2,1)}, bf16[8,64,128]{2,1,0:T(8,128)(2,1)S(1)}, u32[]{:S(2)}) copy-start(bf16[8,64,128]{2,1,0:T(8,128)(2,1)S(1)} %collective-permute-done.6.g) | copy-start | bytes 393220
  55.8 1.0 %copy-start.1 = (f32[9,64,128]{2,1,0:T(8,128)S(1)}, f32[9,64,128]{2,1,0:T(8,128)}, u32[]{:S(2)}) copy-start(f32[9,64,128]{2,1,0:T(8,128)} %copy-done) | copy-start | bytes 884740
  56.7 1.0 %copy-start.3 = (f32[9,64,128]{2,1,0:T(8,128)S(1)}, f32[9,64,128]{2,1,0:T(8,128)}, u32[]{:S(2)}) copy-start(f32[9,64,128]{2,1,0:T(8,128)} %copy-done.2) | copy-start | bytes 884740
  57.7 0.9 %copy-start.6 = (bf16[8,64,128]{2,1,0:T(8,128)(2,1)S(1)}, bf16[8,64,128]{2,1,0:T(8,128)(2,1)}, u32[]{:S(2)}) copy-start(bf16[8,64,128]{2,1,0:T(8,128)(2,1)} %copy-done.5) | copy-start | bytes 393220
